TPU v7x, 256 devices: a whole 4x4x8 slice. The times are simulated.
256 devices in a mesh: pts: 128 (over z_hi, y, x, core), ch: 2 (over z_lo).
Axes of the slice: x: 4, y: 4, z: 8 (z_hi: 4, z_lo: 2; z = z_hi * 2 + z_lo), core: 2. Of those that a mesh axis runs over, the one named last changes fastest.
Arguments:
- points: bfloat16 [524288, 256], P('pts', 'ch'), may hold values from -6 to 6
- order: int32 [524288], P('pts'), may hold values from 0 to 4095, as said below
- norm_gain: float32 [256], P('ch'), may hold values from 0.4 to 12
- qkv_weight: bfloat16 [3, 256, 256], replicated, may hold values from -0.375 to 0.375
- out_weight: bfloat16 [256, 256], replicated, may hold values from -0.375 to 0.375
- tree_gain: float32 [4, 256], P(None, 'ch'), may hold values from 0.3 to 1.5
- partner_slot: int32 [2048, 4], P('pts'), may hold values from 0 to 15
- cotangent: bfloat16 [524288, 256], P('pts', 'ch'), may hold values from -6 to 6
Outputs:
- mixed: bfloat16 [524288, 256], P('pts', 'ch')
- point_grad: bfloat16 [524288, 256], P('pts', 'ch')
- qkv_grad: float32 [3, 256, 256], P(None, None, 'ch')
- out_grad: float32 [256, 256], P('ch')
Inputs may be any that keep to these rules, and one draw needn't show every extreme that they name: `order`: each aligned block of 4096 entries is a permutation of 0 to 4095.
All inputs are finite; a program needn't handle non-finite values.
Results may differ from a plain program's by a relative error of at most 0.015.
The roundings to bfloat16 on the way count: a program that leaves them out, or rounds other values in their place, can miss the bound.
Values may be sent and summed in bfloat16 or wider, within the bound.
A program may use at most 128 MiB of HBM per device.

v0:
```python
import math

import jax
import jax.numpy as jnp
from jax import lax
from jax.sharding import PartitionSpec as P

HEAD = 32
BALL = 256
LEVELS = 4


EPSILON = 1e-06


def swapped(block, axis, distance):
    count = lax.axis_size(axis)
    route = []
    for low in range(count):
        high = low | 1 << distance
        if high != low and high < count:
            route += [(low, high), (high, low)]
    return lax.ppermute(block, axis, route)


def silu_slope(values):
    sigma = jax.nn.sigmoid(values)
    return sigma * (1.0 + values * (1.0 - sigma))


def to_heads(rows_in, group_balls):
    return rows_in.reshape(group_balls, BALL, -1, HEAD)


def group_layout(row_count):
    group_balls = math.gcd(row_count // BALL, 4)
    return (group_balls, row_count // (group_balls * BALL))


def ball_probs(queries, keyset):
    scores = jnp.einsum(
        "bqhd,bkhd->bhqk", queries, keyset, preferred_element_type=jnp.float32
    ) * HEAD ** (-0.5)
    shifted = scores - jnp.max(scores, axis=-1, keepdims=True)
    weights = jnp.exp(shifted)
    return weights / jnp.sum(weights, axis=-1, keepdims=True)


def attention_forward(query_rows, key_rows, value_rows):
    row_count, local_width = query_rows.shape
    group_balls, groups = group_layout(row_count)

    def one_group(triple):
        queries, keyset, values_in = [to_heads(member, group_balls) for member in triple]
        probs_half = ball_probs(queries, keyset).astype(jnp.bfloat16)
        result = jnp.einsum(
            "bhqk,bkhd->bqhd", probs_half, values_in, preferred_element_type=jnp.float32
        )
        return result.astype(jnp.bfloat16).reshape(group_balls * BALL, local_width)

    grouped = tuple(
        (member.reshape(groups, -1, local_width) for member in (query_rows, key_rows, value_rows))
    )
    return lax.map(one_group, grouped).reshape(row_count, local_width)


def attention_backward(query_rows, key_rows, value_rows, grad_rows):
    row_count, local_width = query_rows.shape
    group_balls, groups = group_layout(row_count)

    def one_group(quad):
        queries, keyset, values_in, grad_heads = [to_heads(member, group_balls) for member in quad]
        probs = ball_probs(queries, keyset)
        probs_half = probs.astype(jnp.bfloat16)
        probs_grad = jnp.einsum(
            "bqhd,bkhd->bhqk", grad_heads, values_in, preferred_element_type=jnp.float32
        )
        value_grad = jnp.einsum(
            "bhqk,bqhd->bkhd", probs_half, grad_heads, preferred_element_type=jnp.float32
        )
        score_grad = probs * (probs_grad - jnp.sum(probs_grad * probs, axis=-1, keepdims=True))
        score_half = (score_grad * HEAD ** (-0.5)).astype(jnp.bfloat16)
        query_grad = jnp.einsum(
            "bhqk,bkhd->bqhd", score_half, keyset, preferred_element_type=jnp.float32
        )
        key_grad = jnp.einsum(
            "bhqk,bqhd->bkhd", score_half, queries, preferred_element_type=jnp.float32
        )
        group_rows = group_balls * BALL
        return tuple(
            (
                member.astype(jnp.bfloat16).reshape(group_rows, local_width)
                for member in (query_grad, key_grad, value_grad)
            )
        )

    grouped = tuple(
        (
            member.reshape(groups, -1, local_width)
            for member in (query_rows, key_rows, value_rows, grad_rows)
        )
    )
    outputs = lax.map(one_group, grouped)
    return tuple((member.reshape(row_count, local_width) for member in outputs))


def contract_rows(left, right):
    return lax.dot_general(
        left, right, (((0,), (0,)), ((), ())), preferred_element_type=jnp.float32
    )


def contract_cols(left, right):
    return lax.dot_general(
        left, right, (((1,), (1,)), ((), ())), preferred_element_type=jnp.float32
    )


def sum_out_early(out_term):
    return lax.psum(out_term, "pts")


def local(points, order, norm_gain, qkv_weight, out_weight, tree_gain, partner_slot, cotangent):
    row_count, local_width = points.shape
    balls_here = row_count // BALL
    col_start = lax.axis_index("ch") * local_width
    total_width = local_width * lax.axis_size("ch")
    taken = jnp.take(points, order, axis=0)
    ordered = taken.astype(jnp.float32)
    squares = lax.psum(jnp.sum(ordered * ordered, axis=-1), "ch")
    inverse_rms = lax.rsqrt(squares / total_width + EPSILON)[:, None]
    normed = (ordered * inverse_rms * norm_gain).astype(jnp.bfloat16)
    normed_full = lax.all_gather(normed, "ch", axis=1, tiled=True)
    weight_cols = lax.dynamic_slice_in_dim(qkv_weight, col_start, local_width, 2)
    projected = [
        jnp.dot(normed_full, weight_cols[proj_index], preferred_element_type=jnp.float32).astype(
            jnp.bfloat16
        )
        for proj_index in range(3)
    ]
    attended = attention_forward(projected[0], projected[1], projected[2])
    attended_full = lax.all_gather(attended, "ch", axis=1, tiled=True)
    out_cols = lax.dynamic_slice_in_dim(out_weight, col_start, local_width, 1)
    hidden = ordered + jnp.dot(attended_full, out_cols, preferred_element_type=jnp.float32)
    node_start = hidden.reshape(balls_here, BALL, local_width).sum(axis=1) * BALL ** (-0.5)
    cot_full = cotangent.astype(jnp.float32)
    node_last_grad = cot_full.reshape(balls_here, BALL, local_width).sum(axis=1)
    states = node_start
    chosen_list = []
    for level in range(LEVELS):
        partner_states = swapped(states, "pts", level)
        chosen = jnp.take(partner_states, partner_slot[:, level], axis=0)
        chosen_list.append(chosen)
        states = states + tree_gain[level] * jax.nn.silu(chosen)
    node_grad = node_last_grad
    slot_ids = jnp.arange(balls_here, dtype=jnp.int32)
    for level in reversed(range(LEVELS)):
        terms = tree_gain[level] * silu_slope(chosen_list[level]) * node_grad
        hits = (partner_slot[:, level][:, None] == slot_ids[None, :]).astype(jnp.float32)
        returned = jnp.sum(hits[:, :, None] * terms[:, None, :], axis=0)
        node_grad = node_grad + swapped(returned, "pts", level)
    mixed = (hidden.reshape(balls_here, BALL, local_width) + states[:, None, :]).reshape(
        row_count, local_width
    )
    mixed = mixed.astype(jnp.bfloat16)
    hidden_grad = cot_full.reshape(balls_here, BALL, local_width) + node_grad[
        :, None, :
    ] * BALL ** (-0.5)
    hidden_grad = hidden_grad.reshape(row_count, local_width).astype(jnp.bfloat16)
    hidden_grad_full = lax.all_gather(hidden_grad, "ch", axis=1, tiled=True)
    out_rows = lax.dynamic_slice_in_dim(out_weight, col_start, local_width, 0)
    out_term = sum_out_early(contract_rows(attended, hidden_grad_full))
    attended_grad = contract_cols(hidden_grad_full, out_rows).astype(jnp.bfloat16)
    grads = attention_backward(projected[0], projected[1], projected[2], attended_grad)
    grads_full = (
        lax.all_gather(grads[0], "ch", axis=1, tiled=True),
        lax.all_gather(grads[1], "ch", axis=1, tiled=True),
        lax.all_gather(grads[2], "ch", axis=1, tiled=True),
    )
    qkv_term = jnp.stack([contract_rows(normed_full, grads[proj_index]) for proj_index in range(3)])
    weight_rows = lax.dynamic_slice_in_dim(qkv_weight, col_start, local_width, 1)
    normed_grad = sum(
        (contract_cols(grads_full[proj_index], weight_rows[proj_index]) for proj_index in range(3))
    )
    correction = lax.psum(jnp.sum(ordered * norm_gain * normed_grad, axis=-1), "ch")
    ordered_grad = (
        hidden_grad.astype(jnp.float32)
        + inverse_rms * norm_gain * normed_grad
        - ordered * inverse_rms**3 * correction[:, None] / total_width
    )
    point_grad = jnp.zeros_like(points).at[order].set(ordered_grad.astype(jnp.bfloat16))
    qkv_total = lax.psum(qkv_term, "pts")
    return (mixed, point_grad, qkv_total, out_term)


def solution(mesh):
    in_specs = (
        P("pts", "ch"),
        P("pts"),
        P("ch"),
        P(),
        P(),
        P(None, "ch"),
        P("pts", None),
        P("pts", "ch"),
    )
    out_specs = (P("pts", "ch"), P("pts", "ch"), P(None, None, "ch"), P("ch", None))
    return jax.shard_map(local, mesh=mesh, in_specs=in_specs, out_specs=out_specs, check_vma=False)
```

profile of v0, /device:TPU:1, one launch (start us, length us, event | category | flops | bytes accessed | tf_op | source)
XLA Modules:
  0.0 1875.4 jit_solution(8973191951110241106)
XLA Ops:
  9.4 12.1 gather_fusion
  22.8 7.4 psum.28
  34.6 42.4 %all-gather.7.cloned.1.call-done = bf16[4096,256]{1,0:T(8,128)(2,1)} async-done(((bf16[4096,128]{1,0:T(8,128)(2,1)}), bf16[4096,256]{1,0:T(8,128)(2,1)}) %all-gather.7.cloned.1.call-update) | async-done | bytes 2097168 | tf_op jit(solution)/shard_map/all_gather | solution.py:133
  91.8 65.8 %while.24 = (s32[]{:T(128)}, bf16[4,1024,128]{2,1,0:T(8,128)(2,1)}, bf16[4,1024,128]{1,2,0:T(8,128)(2,1)}, bf16[4,1024,128]{1,2,0:T(8,128)(2,1)}, bf16[4,1024,128]{1,2,0:T(8,128)(2,1)}, /*index=5*/s32[]{:T(128)}) while((s32[]{:T(128)}, bf16[4,1024,128]{2,1,0:T(8,128)(2,1)}, bf16[4,1024,128]{1,2,0:T(8,128)(2,1)}, ...), condition=%wide.region_5.6_spmd, body=%wide.region_2.0_spmd.sunk | while | flops 139591936 | bytes 15761525 | solution.py:64
  131.0 4.6 fusion.176
  147.5 4.6 fusion.176
  159.2 37.2 %all-gather.9.cloned.1.call-done = bf16[4096,256]{1,0:T(8,128)(2,1)} async-done(((bf16[4096,128]{1,0:T(8,128)(2,1)}), bf16[4096,256]{1,0:T(8,128)(2,1)}) %all-gather.9.cloned.1.call-update) | async-done | bytes 2097168 | tf_op jit(solution)/shard_map/all_gather | solution.py:142
  223.2 7.3 collective-permute-start.7
  233.8 38.4 %all-gather.11.cloned.1.call-done = bf16[4096,256]{1,0:T(8,128)(2,1)} async-done(((bf16[4096,128]{1,0:T(8,128)(2,1)}), bf16[4096,256]{1,0:T(8,128)(2,1)}) %all-gather.11.cloned.1.call-update) | async-done | bytes 2097168 | tf_op jit(solution)/shard_map/all_gather | solution.py:170
  278.9 211.6 %while.25 = (s32[]{:T(128)}, bf16[4,1024,128]{2,1,0:T(8,128)(2,1)}, bf16[4,1024,128]{2,1,0:T(8,128)(2,1)}, bf16[4,1024,128]{2,1,0:T(8,128)(2,1)}, bf16[4,1024,12...) while((s32[]{:T(128)}, bf16[4,1024,128]{2,1,0:T(8,128)(2,1)}, ...), condition=%wide.region_16.18_spmd, body=%wide.region_12.17_spmd.sunk | while | flops 355869440 | bytes 43057276 | solution.py:103
  298.9 7.9 fusion.192
  306.8 7.9 fusion.190
  351.8 7.9 fusion.192
  359.7 7.9 fusion.190
  404.7 7.9 fusion.192
  412.6 7.9 fusion.190
  457.6 7.9 fusion.192
  465.5 7.9 fusion.190
  500.4 29.0 %all-gather.13.cloned.1.call-done = bf16[4096,256]{1,0:T(8,128)(2,1)} async-done(((bf16[4096,128]{1,0:T(8,128)(2,1)}), bf16[4096,256]{1,0:T(8,128)(2,1)}) %all-gather.13.cloned.1.call-update) | async-done | bytes 2097168 | tf_op jit(solution)/shard_map/all_gather | solution.py:176
  533.0 36.7 %all-gather.15.cloned.1.call-done = bf16[4096,256]{1,0:T(8,128)(2,1)} async-done(((bf16[4096,128]{1,0:T(8,128)(2,1)}), bf16[4096,256]{1,0:T(8,128)(2,1)}) %all-gather.15.cloned.1.call-update) | async-done | bytes 2097168 | tf_op jit(solution)/shard_map/all_gather | solution.py:177
  573.9 36.0 %all-gather.17.cloned.1.call-done = bf16[4096,256]{1,0:T(8,128)(2,1)} async-done(((bf16[4096,128]{1,0:T(8,128)(2,1)}), bf16[4096,256]{1,0:T(8,128)(2,1)}) %all-gather.17.cloned.1.call-update) | async-done | bytes 2097168 | tf_op jit(solution)/shard_map/all_gather | solution.py:178
  614.4 5.6 psum.29
  620.0 16.8 scatter_custom_fusion
  636.8 1228.5 %all-reduce.3.cloned.1.call-done = (f32[3,256,128]{2,1,0:T(8,128)}, f32[128,256]{1,0:T(8,128)}) async-done(((f32[3,256,128]{2,1,0:T(8,128)}, f32[128,256]{1,0:T(8,128)}), (f32[3,256,128]{2,1,0:T(8,128)}, f32[128,256]{1,0:T(8,128)})) %all-reduce.3.cloned.1.call-update) | async-done | bytes 524304 | tf_op jit(solution)/shard_map/psum | solution.py:192
  (265 shorter events, 291.2 us)
Async XLA Ops:
  7.2 69.9 %all-gather.7.cloned.1.call-start = ((), (), s32[]{:S(2)}) async-start(), calls=%async_computation | async-start | bytes 3145728 | tf_op jit(solution)/shard_map/all_gather | solution.py:133
  9.3 21.5 %copy-start.16 = (f32[128]{0:T(128)S(1)}, f32[128]{0:T(128)}, u32[]{:S(2)}) copy-start(f32[128]{0:T(128)} %param.16) | copy-start | bytes 1540
  21.5 13.1 copy-start.2
  21.5 55.6 %copy-start.11 = (bf16[3,256,256]{2,1,0:T(8,128)(2,1)S(1)}, bf16[3,256,256]{2,1,0:T(8,128)(2,1)}, u32[]{:S(2)}) copy-start(bf16[3,256,256]{2,1,0:T(8,128)(2,1)} %param.17) | copy-start | bytes 1179652
  30.8 46.3 %copy-start.13 = (f32[4096]{0:T(1024)}, f32[4096]{0:T(1024)S(1)}, u32[]{:S(2)}) copy-start(f32[4096]{0:T(1024)S(1)} %get-tuple-element.170) | copy-start | bytes 49156
  34.6 161.8 %all-gather.9.cloned.1.call-start = ((), (), s32[]{:S(2)}) async-start(), calls=%async_computation.1 | async-start | bytes 3145728 | tf_op jit(solution)/shard_map/all_gather | solution.py:142
  157.6 38.8 %copy-start.14 = (bf16[256,256]{1,0:T(8,128)(2,1)S(1)}, bf16[256,256]{1,0:T(8,128)(2,1)}, u32[]{:S(2)}) copy-start(bf16[256,256]{1,0:T(8,128)(2,1)} %param.18) | copy-start | bytes 393220
  157.6 114.6 %all-gather.11.cloned.1.call-start = ((), (), s32[]{:S(2)}) async-start(), calls=%async_computation.2 | async-start | bytes 3145728 | tf_op jit(solution)/shard_map/all_gather | solution.py:170
  199.6 1.5 collective-permute-start
  201.8 2.6 collective-permute-start.1
  205.0 4.1 collective-permute-start.2
  209.8 2.6 collective-permute-start.3
  213.1 2.6 collective-permute-start.4
  216.0 4.1 collective-permute-start.5
  220.2 2.8 collective-permute-start.6
  223.2 8.1 collective-permute-start.7
  233.8 295.6 %all-gather.13.cloned.1.call-start = ((), (), s32[]{:S(2)}) async-start(), calls=%async_computation.3 | async-start | bytes 3145728 | tf_op jit(solution)/shard_map/all_gather | solution.py:176
  490.5 79.1 %all-gather.15.cloned.1.call-start = ((), (), s32[]{:S(2)}) async-start(), calls=%async_computation.4 | async-start | bytes 3145728 | tf_op jit(solution)/shard_map/all_gather | solution.py:177
  491.1 118.8 %all-gather.17.cloned.1.call-start = ((), (), s32[]{:S(2)}) async-start(), calls=%async_computation.5 | async-start | bytes 3145728 | tf_op jit(solution)/shard_map/all_gather | solution.py:178
  491.7 1373.6 %all-reduce.3.cloned.1.call-start = ((), (), s32[]{:S(2)}) async-start(), calls=%async_computation.6 | async-start | bytes 1048576 | tf_op jit(solution)/shard_map/psum | solution.py:192
  499.2 30.2 %copy-start.12 = (bf16[3,256,256]{2,1,0:T(8,128)(2,1)S(1)}, bf16[3,256,256]{2,1,0:T(8,128)(2,1)}, u32[]{:S(2)}) copy-start(bf16[3,256,256]{2,1,0:T(8,128)(2,1)} %param.17) | copy-start | bytes 1179652
  533.0 77.0 %copy-start.3 = (bf16[4096,128]{1,0:T(8,128)(2,1)S(1)}, bf16[4096,128]{1,0:T(8,128)(2,1)}, u32[]{:S(2)}) copy-start(bf16[4096,128]{1,0:T(8,128)(2,1)} %copy-done.2) | copy-start | bytes 3145732
  533.0 77.0 %copy-start.17 = (f32[128]{0:T(128)S(1)}, f32[128]{0:T(128)}, u32[]{:S(2)}) copy-start(f32[128]{0:T(128)} %param.16) | copy-start | bytes 1540
  573.9 46.0 %copy-start.9 = (bf16[4096,128]{1,0:T(8,128)(2,1)S(1)}, bf16[4096,128]{1,0:T(8,128)(2,1)}, u32[]{:S(2)}) copy-start(bf16[4096,128]{1,0:T(8,128)(2,1)} %fusion.93) | copy-start | bytes 3145732
  (13 other events, 34.7 us)
Sparse Core Ops, SparseCore 0:
  34.7 42.3 all-gather.6
  157.7 38.6 all-gather.8
  233.9 38.2 all-gather.10
  490.6 38.6 all-gather.12
  531.0 38.6 all-gather.14
  571.3 38.6 all-gather.16
  613.2 1251.9 all-reduce.2
where the time goes:
time: 1880 us
  waiting for transfers between devices  1460 us (78%)
  local copies, waits for them, and re-layouts  172 us (9%)
  matrix products  165 us (9%)
  other arithmetic  33.3 us (2%)
  starting transfers between devices  19.3 us (1%)
    psum x1, waiting for transfers between devices, local(): qkv_total = lax.psum(qkv_term, 'pts')  1230 us
    all_gather x1, waiting for transfers between devices, local(): normed_full = lax.all_gather(normed, 'ch', axis=1, tiled=True)  42.4 us
    all_gather x1, waiting for transfers between devices, local(): hidden_grad_full = lax.all_gather(hidden_grad, 'ch', axis=1, tiled=True)  38.4 us
  transfers between devices with their start and end apart: 15, of which 15 were waited for; matrix products, arithmetic and copies ran while one was open for 2% of the time, Pallas kernels for 0%

commit v1 on v0

v1 whole, which is shorter than its diff:
```python
import math

import jax
import jax.numpy as jnp
from jax import lax
from jax.experimental import pallas as pl
from jax.experimental.pallas import tpu as pltpu
from jax.sharding import PartitionSpec as P

HEAD = 32
BALL = 256
LEVELS = 4
EPSILON = 1e-06

ROWS = 4096
HALF = 2048
LOCAL = 128
WIDTH = 256
HEADS = 8
BALLS = 8
GROUP = 16

F32 = jnp.float32
BF16 = jnp.bfloat16
MESH = pl.DeviceIdType.MESH
SCALE = HEAD ** (-0.5)
SCALE_LOG2 = SCALE * math.log2(math.e)


def nn(left, right):
    return lax.dot_general(left, right, (((1,), (0,)), ((), ())), preferred_element_type=F32)


def nt(left, right):
    return lax.dot_general(left, right, (((1,), (1,)), ((), ())), preferred_element_type=F32)


def tn(left, right):
    return lax.dot_general(left, right, (((0,), (0,)), ((), ())), preferred_element_type=F32)


def gather_kernel(order_ref, points_ref, out_ref, wide, moved):
    wide[...] = points_ref[...].astype(F32)

    def step(block, carry):
        base = block * 16
        for inner in range(16):
            row = order_ref[base + inner]
            moved[pl.ds(base + inner, 1), :] = wide[pl.ds(row, 1), :]
        return carry

    lax.fori_loop(0, ROWS // 16, step, 0)
    out_ref[...] = moved[...].astype(BF16)


def scatter_kernel(order_ref, rows_ref, out_ref, wide, moved):
    wide[...] = rows_ref[...].astype(F32)

    def step(block, carry):
        base = block * 16
        for inner in range(16):
            row = order_ref[base + inner]
            moved[pl.ds(row, 1), :] = wide[pl.ds(base + inner, 1), :]
        return carry

    lax.fori_loop(0, ROWS // 16, step, 0)
    out_ref[...] = moved[...].astype(BF16)


def permute_rows(kernel, order, rows):
    return pl.pallas_call(
        kernel,
        out_shape=jax.ShapeDtypeStruct((ROWS, LOCAL), BF16),
        in_specs=[pl.BlockSpec(memory_space=pltpu.SMEM), pl.BlockSpec(memory_space=pltpu.VMEM)],
        out_specs=pl.BlockSpec(memory_space=pltpu.VMEM),
        scratch_shapes=[pltpu.VMEM((ROWS, LOCAL), F32), pltpu.VMEM((ROWS, LOCAL), F32)],
        compiler_params=pltpu.CompilerParams(vmem_limit_bytes=24 * 1024 * 1024),
    )(order, rows)


def exact_dot(dot, onehot, values):
    high = values.astype(BF16)
    rest = values - high.astype(F32)
    middle = rest.astype(BF16)
    low = (rest - middle.astype(F32)).astype(BF16)
    return dot(onehot, high) + dot(onehot, middle) + dot(onehot, low)


def main_kernel(
    gathered, cot, small, slots, w, wo,
    mixed, grads, total,
    xh, cth, sm, wt, kn, vn, q_t, k_t, v_t, att_t, nrm, hid, inv, probs, dx,
    tree, final_state, final_grad, mstage, gstage, acc_t,
    acc, recv_a, sum_a, recv_b, sum_b, recv_c, sum_c, recv_d, sum_d, all_e, all_f,
    s_small, s_pts, s_cot, s_mix, s_grad, s_tree, s_a, s_b, s_c, s_d, s_e, s_f, s_g,
):
    p = lax.axis_index("pts")
    c = lax.axis_index("ch")
    core = p % 2
    plane = (p // 2) % 16
    depth = p // 32
    other_c = 1 - c
    me = (p % GROUP) * 2 + c
    group_base = (p // GROUP) * GROUP
    pair = (p, other_c)
    sibling = (p + 1 - 2 * core, c)

    def tree_peer(distance):
        there = (me + distance) % 32
        return (group_base + there // 2, there % 2)

    def plane_index(distance):
        return (plane + distance) % 16

    def plane_peer(distance):
        return (depth * 32 + plane_index(distance) * 2 + core, c)

    def depth_index(distance):
        return (depth + distance) % 4

    def depth_peer(distance):
        return (depth_index(distance) * 32 + plane * 2 + core, c)

    barrier = pltpu.get_barrier_semaphore()
    for distance in range(1, 32):
        pl.semaphore_signal(barrier, inc=1, device_id=tree_peer(distance), device_id_type=MESH)
    far_base = (1 - plane // 8) * 8
    for step in range(8):
        far = (depth * 32 + (far_base + step) * 2 + core, c)
        pl.semaphore_signal(barrier, inc=1, device_id=far, device_id_type=MESH)
    for distance in range(1, 4):
        pl.semaphore_signal(barrier, inc=1, device_id=depth_peer(distance), device_id_type=MESH)

    own_rows = pl.ds(pl.multiple_of(c * HALF, HALF), HALF)
    xh[pl.ds(c, 1)] = gathered[own_rows, :][None]
    cth[pl.ds(c, 1)] = cot[own_rows, :][None]
    sm[pl.ds(c, 1)] = small[...][None]
    for index in range(3):
        wt[index] = jnp.transpose(w[index])

    pl.semaphore_wait(barrier, 42)

    def send(src, dst, sems, index, target):
        return pltpu.make_async_remote_copy(
            src_ref=src, dst_ref=dst, send_sem=sems.at[0, index], recv_sem=sems.at[1, index],
            device_id=target, device_id_type=MESH,
        )

    def theirs(ball):
        return pl.ds(pl.multiple_of(other_c * HALF + ball * BALL, BALL), BALL)

    def ours(ball):
        return pl.ds(pl.multiple_of(c * HALF + ball * BALL, BALL), BALL)

    def here(ball):
        return pl.ds(pl.multiple_of(ball * BALL, BALL), BALL)

    def small_copy():
        return send(small, sm.at[c], s_small, 0, pair)

    def points_copy(ball):
        return send(gathered.at[theirs(ball)], xh.at[c, here(ball)], s_pts, ball, pair)

    def cot_copy(ball):
        return send(cot.at[theirs(ball)], cth.at[c, here(ball)], s_cot, ball, pair)

    def mixed_copy(ball):
        return send(mstage.at[other_c, here(ball)], mixed.at[ours(ball)], s_mix, ball, pair)

    def grad_copy(ball):
        return send(gstage.at[other_c, here(ball)], grads.at[ours(ball)], s_grad, ball, pair)

    small_copy().start()
    for ball in range(BALLS):
        points_copy(ball).start()
    small_copy().wait_recv()
    gain = jnp.concatenate([sm[0, 0:1, :], sm[1, 0:1, :]], axis=1)

    node_row = pl.multiple_of(me * BALLS, BALLS)

    def both(ref, rows):
        return jnp.concatenate([ref[0, rows, :], ref[1, rows, :]], axis=1).astype(F32)

    def forward(ball, carry):
        rows = here(ball)
        points_copy(ball).wait_recv()
        cot_copy(ball).start()
        ordered = both(xh, rows)
        mean = jnp.sum(ordered * ordered, axis=1, keepdims=True) * (1.0 / WIDTH)
        inverse = lax.rsqrt(mean + EPSILON)
        inv[rows, :] = jnp.broadcast_to(inverse, (BALL, LOCAL))
        normed = (ordered * inverse * gain).astype(BF16)
        nrm[rows, :] = normed
        keyset = nn(normed, w[1]).astype(BF16)
        kn[rows, :] = keyset
        vn[rows, :] = nn(normed, w[2]).astype(BF16)
        q_t[ball] = nt(wt[0], normed).astype(BF16)
        k_t[ball] = nt(wt[1], normed).astype(BF16)
        v_t[ball] = nt(wt[2], normed).astype(BF16)
        for head in range(HEADS):
            cols = slice(head * HEAD, (head + 1) * HEAD)
            scores = nn(kn[rows, cols], q_t[ball, cols, :])
            top = jnp.max(scores, axis=0, keepdims=True)
            weights = jnp.exp2((scores - top) * SCALE_LOG2)
            scaled = weights * (1.0 / jnp.sum(weights, axis=0, keepdims=True))
            probs[ball * HEADS + head] = scaled
            att_t[ball, cols, :] = nn(v_t[ball, cols, :], scaled.astype(BF16)).astype(BF16)
        hidden = ordered + nn(jnp.transpose(att_t[ball]), wo[...])
        hid[rows, :] = hidden
        tree[pl.ds(node_row + ball, 1), 0:WIDTH] = jnp.sum(hidden, axis=0, keepdims=True) * BALL ** (-0.5)
        return carry

    lax.fori_loop(0, BALLS, forward, 0)

    for ball in range(BALLS):
        cot_copy(ball).wait_recv()
        tree[pl.ds(node_row + ball, 1), WIDTH:2 * WIDTH] = jnp.sum(
            both(cth, here(ball)), axis=0, keepdims=True
        )
    tree[pl.ds(node_row, BALLS), 2 * WIDTH:] = slots[pl.ds(pl.multiple_of(c * BALLS, BALLS), BALLS), :]

    def tree_copy(distance):
        block = tree.at[pl.ds(node_row, BALLS)]
        return send(block, block, s_tree, distance, tree_peer(distance))

    for distance in range(1, 32):
        tree_copy(distance).start()
    for distance in range(1, 32):
        tree_copy(distance).wait_recv()

    nodes = GROUP * 16
    range_ids = lax.broadcasted_iota(jnp.int32, (nodes, 1), 0) // 16
    lane_ids = lax.broadcasted_iota(jnp.int32, (nodes, nodes), 1)
    states = tree[:, 0:WIDTH]
    onehots, chosen_list, tree_gains = [], [], []
    for level in range(LEVELS):
        slot = tree[:, 2 * WIDTH + level:2 * WIDTH + level + 1].astype(jnp.int32)
        bit = (range_ids // (1 << level)) % 2
        partner = (range_ids + (1 - 2 * bit) * (1 << level)) * 16 + slot
        onehot = jnp.where(lane_ids == partner, 1.0, 0.0).astype(BF16)
        tree_gain = jnp.concatenate([sm[0, 1 + level:2 + level, :], sm[1, 1 + level:2 + level, :]], axis=1)
        chosen = exact_dot(nn, onehot, states)
        states = states + tree_gain * (chosen * jax.nn.sigmoid(chosen))
        onehots.append(onehot)
        chosen_list.append(chosen)
        tree_gains.append(tree_gain)
    final_state[...] = states
    node_grad = tree[:, WIDTH:2 * WIDTH]
    for level in reversed(range(LEVELS)):
        chosen = chosen_list[level]
        sigma = jax.nn.sigmoid(chosen)
        slope = sigma * (1.0 + chosen * (1.0 - sigma))
        node_grad = node_grad + exact_dot(tn, onehots[level], tree_gains[level] * slope * node_grad)
    final_grad[...] = node_grad
    acc_t[...] = jnp.zeros_like(acc_t)

    def backward(ball, carry):
        rows = here(ball)
        mixed_rows = (hid[rows, :] + final_state[pl.ds(node_row + ball, 1), :]).astype(BF16)
        mstage[0, rows, :] = mixed_rows[:, :LOCAL]
        mstage[1, rows, :] = mixed_rows[:, LOCAL:]
        mixed_copy(ball).start()
        mixed[ours(ball), :] = mstage[pl.ds(c, 1), rows, :][0]
        shift = final_grad[pl.ds(node_row + ball, 1), :] * BALL ** (-0.5)
        hidden_grad = (both(cth, rows) + shift).astype(BF16)
        acc_t[3] += nn(att_t[ball], hidden_grad)
        att_grad = nt(wo[...], hidden_grad).astype(BF16)
        for head in range(HEADS):
            cols = slice(head * HEAD, (head + 1) * HEAD)
            prob = probs[ball * HEADS + head]
            head_grad = att_grad[cols, :]
            prob_grad = nn(vn[rows, cols], head_grad)
            dx[2, cols, :] = nt(head_grad, prob.astype(BF16)).astype(BF16)
            dots = jnp.sum(prob_grad * prob, axis=0, keepdims=True)
            score_grad = (prob * (prob_grad - dots) * SCALE).astype(BF16)
            dx[0, cols, :] = nn(k_t[ball, cols, :], score_grad).astype(BF16)
            dx[1, cols, :] = nt(q_t[ball, cols, :], score_grad).astype(BF16)
        normed = nrm[rows, :]
        for index in range(3):
            acc_t[index] += nn(dx[index], normed)
        normed_grad = nn(w[0], dx[0]) + nn(w[1], dx[1]) + nn(w[2], dx[2])
        scaled_grad = jnp.transpose(normed_grad) * gain
        ordered = both(xh, rows)
        inverse = jnp.concatenate([inv[rows, :], inv[rows, :]], axis=1)
        correction = jnp.sum(ordered * scaled_grad, axis=1, keepdims=True) * (1.0 / WIDTH)
        ordered_grad = (
            hidden_grad.astype(F32) + inverse * scaled_grad - ordered * (inverse * inverse * inverse) * correction
        ).astype(BF16)
        gstage[0, rows, :] = ordered_grad[:, :LOCAL]
        gstage[1, rows, :] = ordered_grad[:, LOCAL:]
        grad_copy(ball).start()
        grads[ours(ball), :] = gstage[pl.ds(c, 1), rows, :][0]
        return carry

    lax.fori_loop(0, BALLS, backward, 0)

    for index in range(3):
        part = jnp.transpose(acc_t[index])
        acc[0, index * 256:(index + 1) * 256, :] = part[:, :LOCAL]
        acc[1, index * 256:(index + 1) * 256, :] = part[:, LOCAL:]
    for half in range(2):
        band = slice(half * LOCAL, (half + 1) * LOCAL)
        acc[half, 768:896, :] = acc_t[3, band, :LOCAL]
        acc[half, 896:1024, :] = acc_t[3, band, LOCAL:]

    kept = pl.ds(pl.multiple_of(core * 512, 512), 512)
    given = pl.ds(pl.multiple_of((1 - core) * 512, 512), 512)
    copy_a = send(acc.at[:, given], recv_a, s_a, 0, sibling)
    copy_a.start()
    copy_a.wait_recv()
    sum_a[...] = acc[:, kept, :] + recv_a[...]
    copy_b = send(sum_a.at[other_c], recv_b, s_b, 0, pair)
    copy_b.start()
    copy_b.wait_recv()
    sum_b[...] = sum_a[pl.ds(c, 1)][0] + recv_b[...]

    def copy_c(distance):
        piece = pl.ds(pl.multiple_of(plane_index(distance) * 32, 32), 32)
        return send(sum_b.at[piece], recv_c.at[distance], s_c, distance, plane_peer(distance))

    for distance in range(1, 16):
        copy_c(distance).start()
    part = sum_b[pl.ds(pl.multiple_of(plane * 32, 32), 32), :]
    for distance in range(1, 16):
        copy_c(distance).wait_recv()
        part = part + recv_c[distance]
    sum_c[...] = part

    def copy_d(distance):
        piece = pl.ds(pl.multiple_of(depth_index(distance) * 8, 8), 8)
        return send(sum_c.at[piece], recv_d.at[distance], s_d, distance, depth_peer(distance))

    for distance in range(1, 4):
        copy_d(distance).start()
    part = sum_c[pl.ds(pl.multiple_of(depth * 8, 8), 8), :]
    for distance in range(1, 4):
        copy_d(distance).wait_recv()
        part = part + recv_d[distance]
    sum_d[...] = part

    depth_rows = pl.ds(pl.multiple_of(depth * 8, 8), 8)
    all_e[depth_rows, :] = part

    def copy_e(distance):
        return send(sum_d, all_e.at[depth_rows], s_e, distance, depth_peer(distance))

    for distance in range(1, 4):
        copy_e(distance).start()
    for distance in range(1, 4):
        copy_e(distance).wait_recv()

    plane_rows = pl.ds(pl.multiple_of(plane * 32, 32), 32)
    all_f[plane_rows, :] = all_e[...]

    def copy_f(distance):
        return send(all_e, all_f.at[plane_rows], s_f, distance, plane_peer(distance))

    for distance in range(1, 16):
        copy_f(distance).start()
    for distance in range(1, 16):
        copy_f(distance).wait_recv()

    copy_g = send(all_f, total.at[kept], s_g, 0, sibling)
    copy_g.start()
    total[kept, :] = all_f[...]
    copy_g.wait_recv()

    small_copy().wait_send()

    def settle(ball, carry):
        points_copy(ball).wait_send()
        cot_copy(ball).wait_send()
        mixed_copy(ball).wait()
        grad_copy(ball).wait()
        return carry

    lax.fori_loop(0, BALLS, settle, 0)
    for distance in range(1, 32):
        tree_copy(distance).wait_send()
    copy_a.wait_send()
    copy_b.wait_send()
    for distance in range(1, 16):
        copy_c(distance).wait_send()
        copy_f(distance).wait_send()
    for distance in range(1, 4):
        copy_d(distance).wait_send()
        copy_e(distance).wait_send()
    copy_g.wait_send()


def run_main(gathered, cot, small, slots, w, wo):
    vmem = pl.BlockSpec(memory_space=pltpu.VMEM)
    sems = lambda count: pltpu.SemaphoreType.DMA((2, count))
    v = pltpu.VMEM
    return pl.pallas_call(
        main_kernel,
        out_shape=(
            jax.ShapeDtypeStruct((ROWS, LOCAL), BF16),
            jax.ShapeDtypeStruct((ROWS, LOCAL), BF16),
            jax.ShapeDtypeStruct((1024, LOCAL), F32),
        ),
        in_specs=[vmem] * 6,
        out_specs=(vmem,) * 3,
        scratch_shapes=[
            v((2, HALF, LOCAL), BF16),
            v((2, HALF, LOCAL), BF16),
            v((2, 8, LOCAL), F32),
            v((3, WIDTH, WIDTH), BF16),
            v((HALF, WIDTH), BF16),
            v((HALF, WIDTH), BF16),
            v((BALLS, WIDTH, BALL), BF16),
            v((BALLS, WIDTH, BALL), BF16),
            v((BALLS, WIDTH, BALL), BF16),
            v((BALLS, WIDTH, BALL), BF16),
            v((HALF, WIDTH), BF16),
            v((HALF, WIDTH), F32),
            v((HALF, LOCAL), F32),
            v((BALLS * HEADS, BALL, BALL), F32),
            v((3, WIDTH, BALL), BF16),
            v((256, 640), F32),
            v((256, WIDTH), F32),
            v((256, WIDTH), F32),
            v((2, HALF, LOCAL), BF16),
            v((2, HALF, LOCAL), BF16),
            v((4, WIDTH, WIDTH), F32),
            v((2, 1024, LOCAL), F32),
            v((2, 512, LOCAL), F32),
            v((2, 512, LOCAL), F32),
            v((512, LOCAL), F32),
            v((512, LOCAL), F32),
            v((16, 32, LOCAL), F32),
            v((32, LOCAL), F32),
            v((4, 8, LOCAL), F32),
            v((8, LOCAL), F32),
            v((32, LOCAL), F32),
            v((512, LOCAL), F32),
            sems(1), sems(BALLS), sems(BALLS), sems(BALLS), sems(BALLS), sems(32),
            sems(1), sems(1), sems(16), sems(4), sems(4), sems(16), sems(1),
        ],
        compiler_params=pltpu.CompilerParams(
            collective_id=0, has_side_effects=True, vmem_limit_bytes=56 * 1024 * 1024
        ),
        cost_estimate=pl.CostEstimate(flops=8 * 10**9, bytes_accessed=8 * 10**6, transcendentals=4 * 10**6),
    )(gathered, cot, small, slots, w, wo)


def local(points, order, norm_gain, qkv_weight, out_weight, tree_gain, partner_slot, cotangent):
    gathered = permute_rows(gather_kernel, order, points)
    small = jnp.concatenate([norm_gain[None], tree_gain, jnp.zeros((3, LOCAL), F32)], axis=0)
    slots = jnp.pad(partner_slot.astype(F32), ((0, 0), (0, LOCAL - LEVELS)))
    mixed, grads, total = run_main(gathered, cotangent, small, slots, qkv_weight, out_weight)
    point_grad = permute_rows(scatter_kernel, order, grads)
    qkv_total = total[:768].reshape(3, WIDTH, LOCAL)
    out_total = jnp.concatenate([total[768:896], total[896:]], axis=1)
    return (mixed, point_grad, qkv_total, out_total)


def solution(mesh):
    in_specs = (
        P("pts", "ch"),
        P("pts"),
        P("ch"),
        P(),
        P(),
        P(None, "ch"),
        P("pts", None),
        P("pts", "ch"),
    )
    out_specs = (P("pts", "ch"), P("pts", "ch"), P(None, None, "ch"), P("ch", None))
    return jax.shard_map(local, mesh=mesh, in_specs=in_specs, out_specs=out_specs, check_vma=False)
```

time: 1880 us -> 131 us (0.07)
  waiting for transfers between devices: 1460 us -> 0 us
  matrix products: 165 us -> 0 us
  local copies, waits for them, and re-layouts: 172 us -> 7.94 us
  Pallas kernels: 0 us -> 121 us
  other arithmetic: 33.3 us -> 1.33 us
  starting transfers between devices: 19.3 us -> 0 us
    psum x1 -> x0, waiting for transfers between devices: 1230 us -> none  [local(): qkv_total = lax.psum(qkv_term, 'pts')]
    all_gather x6 -> x0, waiting for transfers between devices: 220 us -> none  [the longest x1 42.4 us: local(): normed_full = lax.all_gather(normed, 'ch', axis=1, tiled=True)]
    dot_general x32 -> x0, matrix products: 129 us -> none  [the longest x4 31.7 us: one_group(): jnp.einsum('bhqk,bkhd->bqhd', score_half, keyset, preferred_element_type=...]
    pallas_call x0 -> x3, Pallas kernels: none -> 121 us  [the longest x1 109 us: run_main(): pl.pallas_call(main_kernel, out_shape=(jax.ShapeDtypeStruct((ROWS, LOCAL)...]
    reshape x28 -> x0, local copies, waits for them, and re-layouts: 37.3 us -> none  [to_heads(): return rows_in.reshape(group_balls, BALL, -1, HEAD)]
    dynamic_update_slice x28 -> x0, local copies, waits for them, and re-layouts: 36.6 us -> none  [attention_forward(): return lax.map(one_group, grouped).reshape(row_count, local_width)]
    sub x8 -> x0, matrix products: 36.3 us -> none  [ball_probs(): shifted = scores - jnp.max(scores, axis=-1, keepdims=True)]
    dynamic_slice x28 -> x0, local copies, waits for them, and re-layouts: 35.5 us -> none  [attention_forward(): return lax.map(one_group, grouped).reshape(row_count, local_width)]
  transfers between devices with their start and end apart: 15 -> 0, of which waited for: 15 -> 0; matrix products, arithmetic and copies ran while one was open for 2% -> 0% of each run, Pallas kernels for 0% -> 0%
where the time goes in v1:
time: 131 us
  Pallas kernels  121 us (92%)
  local copies, waits for them, and re-layouts  7.94 us (6%)
  other arithmetic  1.33 us (1%)
    pallas_call x1, Pallas kernels, run_main(): pl.pallas_call(main_kernel, out_shape=(jax.ShapeDtypeStruct((ROWS, LOCAL)...  109 us
    pallas_call x2, Pallas kernels, permute_rows(): pl.pallas_call(kernel, out_shape=jax.ShapeDtypeStruct((ROWS, LOCAL), BF16...  11.8 us
    unnamed x17, local copies, waits for them, and re-layouts  4.44 us

profile of v1, /device:TPU:1, one launch (start us, length us, event | category | flops | bytes accessed | tf_op | source)
XLA Modules:
  0.0 130.6 jit_solution(6143146482528333702)
XLA Ops:
  0.6 0.0 copy-start.6
  0.7 0.1 pad.9.clone
  0.7 0.6 copy-done.6
  1.3 0.0 copy-start.5
  1.3 0.7 copy-done.5
  2.0 0.0 copy-done.7
  2.0 0.0 copy-start.3
  2.0 0.7 maximum_maximum_fusion.small
  2.7 0.1 copy.13
  2.7 0.6 pad.4.slots
  3.4 0.0 copy-done.3
  3.4 1.2 copy-done
  4.6 5.4 %shard_map.111.gathered = bf16[4096,128]{1,0:T(8,128)(2,1)S(1)} custom-call(s32[4096]{0:T(1024)S(1)} %copy-done.3, bf16[4096,128]{1,0:T(8,128)(2,1)S(1)} %copy-done), custom_call_target="tpu_custom_call" | custom-call | tf_op jit(solution)/shard_map/pallas_call | solution.py:71
  9.9 0.0 copy-start.2
  9.9 1.0 copy-done.2
  10.9 108.9 %shard_map.112 = (bf16[4096,128]{1,0:T(8,128)(2,1)}, bf16[4096,128]{1,0:T(8,128)(2,1)}, f32[1024,128]{1,0:T(8,128)}) custom-call(bf16[4096,128]{1,0:T(8,128)(2,1)} %copy-done.2, bf16[4096,128]{1,0:T(8,128)(2,1)} %cot.1, f32[8,128]{1,0:T(8,128)} %maximum_maximum_fusion.small, f32[16,128]{1,0:T(8,128)} %pad.4.slots, bf16[3,256,256]{2,1,0:T(8,128)(2,1)} %w.1, ...), custom_call_target="tpu_custom_call" | custom-call | flops 8000000000 | bytes 8000000 | tf_op jit(solution)/shard_map/pallas_call | solution.py:395
  119.8 0.0 copy-start.1
  119.8 1.0 fusion
  120.8 1.8 %slice.9 = f32[768,128]{1,0:T(8,128)} slice(f32[1024,128]{1,0:T(8,128)} %get-tuple-element.9), slice={[0:768], [0:128]} | slice | bytes 786432 | tf_op jit(solution)/shard_map/slice | solution.py:453
  122.5 0.7 pad_maximum_fusion
  123.2 0.0 copy-done.1
  123.2 6.5 %shard_map.113 = bf16[4096,128]{1,0:T(8,128)(2,1)} custom-call(s32[4096]{0:T(1024)S(1)} %copy-done.3, bf16[4096,128]{1,0:T(8,128)(2,1)S(1)} %copy-done.1), custom_call_target="tpu_custom_call" | custom-call | tf_op jit(solution)/shard_map/pallas_call | solution.py:71
  129.7 0.0 copy-done.4
  129.7 1.0 copy.15
  (5 shorter events, 0.0 us)
Async XLA Ops:
  0.6 0.7 copy-start.6
  1.3 0.7 copy-start.5
  1.3 0.7 copy-start.7
  2.0 1.4 %copy-start.3 = (s32[4096]{0:T(1024)S(1)}, s32[4096]{0:T(1024)}, u32[]{:S(2)}) copy-start(s32[4096]{0:T(1024)} %order_ref.3) | copy-start | bytes 49156
  3.4 1.2 copy-start
  9.9 1.0 copy-start.2
  119.8 3.4 %copy-start.1 = (bf16[4096,128]{1,0:T(8,128)(2,1)S(1)}, bf16[4096,128]{1,0:T(8,128)(2,1)}, u32[]{:S(2)}) copy-start(bf16[4096,128]{1,0:T(8,128)(2,1)} %get-tuple-element.8.rows_ref) | copy-start | bytes 3145732
  123.2 6.5 %copy-start.4 = (bf16[4096,128]{1,0:T(8,128)(2,1)S(1)}, bf16[4096,128]{1,0:T(8,128)(2,1)}, u32[]{:S(2)}) copy-start(bf16[4096,128]{1,0:T(8,128)(2,1)} %get-tuple-element.16) | copy-start | bytes 3145732

commit v2 on v1

v2 whole, which is shorter than its diff:
```python
import math

import jax
import jax.numpy as jnp
from jax import lax
from jax.experimental import pallas as pl
from jax.experimental.pallas import tpu as pltpu
from jax.sharding import PartitionSpec as P

HEAD = 32
BALL = 256
LEVELS = 4
EPSILON = 1e-06

ROWS = 4096
HALF = 2048
LOCAL = 128
WIDTH = 256
HEADS = 8
BALLS = 8
GROUP = 16
EARLY_COT = 4

F32 = jnp.float32
BF16 = jnp.bfloat16
MESH = pl.DeviceIdType.MESH
SCALE = HEAD ** (-0.5)
SCALE_LOG2 = SCALE * math.log2(math.e)


def nn(left, right):
    return lax.dot_general(left, right, (((1,), (0,)), ((), ())), preferred_element_type=F32)


def nt(left, right):
    return lax.dot_general(left, right, (((1,), (1,)), ((), ())), preferred_element_type=F32)


def scatter_kernel(order_ref, rows_ref, out_ref, wide, moved):
    wide[...] = rows_ref[...].astype(F32)

    def step(block, carry):
        base = block * 16
        for inner in range(16):
            row = order_ref[base + inner]
            moved[pl.ds(row, 1), :] = wide[pl.ds(base + inner, 1), :]
        return carry

    lax.fori_loop(0, ROWS // 16, step, 0)
    out_ref[...] = moved[...].astype(BF16)


def permute_rows(kernel, order, rows):
    return pl.pallas_call(
        kernel,
        out_shape=jax.ShapeDtypeStruct((ROWS, LOCAL), BF16),
        in_specs=[pl.BlockSpec(memory_space=pltpu.SMEM), pl.BlockSpec(memory_space=pltpu.VMEM)],
        out_specs=pl.BlockSpec(memory_space=pltpu.VMEM),
        scratch_shapes=[pltpu.VMEM((ROWS, LOCAL), F32), pltpu.VMEM((ROWS, LOCAL), F32)],
        compiler_params=pltpu.CompilerParams(vmem_limit_bytes=24 * 1024 * 1024),
    )(order, rows)


def exact_dot(onehot, values):
    high = values.astype(BF16)
    rest = values - high.astype(F32)
    middle = rest.astype(BF16)
    low = (rest - middle.astype(F32)).astype(BF16)
    parts = nn(onehot, jnp.concatenate([high, middle, low], axis=1))
    return parts[:, :LOCAL] + parts[:, LOCAL:2 * LOCAL] + parts[:, 2 * LOCAL:]


def main_kernel(
    order_ref, points, cot, gain_ref, tree_gain_ref, slots, w, wo,
    mixed, grads, qkv_out, out_out,
    wide, moved, theirs_rows, xh, cth, sm, wt, wcat, vn, q_t, k_t, att_t, nrm, hid, inv, probs,
    early, nodes_own, nodes, picks, picks_t, final_state, final_grad, node_grads,
    pstage, precv, gstage, acc_t,
    acc, recv_a, sum_a, recv_c, sum_c, recv_z, all_f, total,
    s_small, s_pts, s_cot, s_proj, s_grad, s_early, s_tree, s_ng, s_a, s_c, s_z, s_f, s_g,
):
    p = lax.axis_index("pts")
    c = lax.axis_index("ch")
    core = p % 2
    plane = (p // 2) % 16
    depth = p // 32
    other_c = 1 - c
    local_range = p % GROUP
    me = local_range * 2 + c
    group_base = (p // GROUP) * GROUP
    ring = depth * 2 + c
    pair = (p, other_c)
    sibling = (p + 1 - 2 * core, c)

    def tree_peer(distance):
        there = (me + distance) % 32
        return (group_base + there // 2, there % 2)

    def early_peer(distance):
        return (group_base + (local_range + distance) % GROUP, c)

    def plane_index(distance):
        return (plane + distance) % 16

    def plane_peer(distance):
        return (depth * 32 + plane_index(distance) * 2 + core, c)

    def ring_peer(distance):
        there = (ring + distance) % 8
        return ((there // 2) * 32 + plane * 2 + core, there % 2)

    barrier = pltpu.get_barrier_semaphore()

    def greet(target):
        pl.semaphore_signal(barrier, inc=1, device_id=target, device_id_type=MESH)

    for distance in range(1, 32):
        greet(tree_peer(distance))
    far_base = (1 - plane // 8) * 8
    for step in range(8):
        greet((depth * 32 + (far_base + step) * 2 + core, c))
    for step in range(1, 4):
        for half in range(2):
            greet((((depth + step) % 4) * 32 + plane * 2 + core, half))

    def send(src, dst, sems, index, target):
        return pltpu.make_async_remote_copy(
            src_ref=src, dst_ref=dst, send_sem=sems.at[0, index], recv_sem=sems.at[1, index],
            device_id=target, device_id_type=MESH,
        )

    def theirs(ball):
        return pl.ds(pl.multiple_of(other_c * HALF + ball * BALL, BALL), BALL)

    def ours(ball):
        return pl.ds(pl.multiple_of(c * HALF + ball * BALL, BALL), BALL)

    def here(ball):
        return pl.ds(pl.multiple_of(ball * BALL, BALL), BALL)

    def small_copy():
        return send(sm.at[c], sm.at[c], s_small, 0, pair)

    def points_copy(ball):
        return send(theirs_rows.at[here(ball)], xh.at[c, here(ball)], s_pts, ball, pair)

    def cot_copy(ball):
        return send(cot.at[theirs(ball)], cth.at[c, here(ball)], s_cot, ball, pair)

    def proj_copy(ball):
        return send(pstage.at[other_c, here(ball)], precv.at[here(ball)], s_proj, ball, pair)

    def grad_copy(ball):
        return send(gstage.at[other_c, here(ball)], grads.at[ours(ball)], s_grad, ball, pair)

    def both(ref, rows):
        return jnp.concatenate([ref[0, rows, :], ref[1, rows, :]], axis=1).astype(F32)

    wide[...] = points[...].astype(F32)

    def pick_rows(start):
        def step(block, carry):
            base = start + block * 16
            for inner in range(16):
                row = order_ref[base + inner]
                moved[pl.ds(base + inner, 1), :] = wide[pl.ds(row, 1), :]
            return carry

        lax.fori_loop(0, BALL // 16, step, 0)
        return moved[pl.ds(pl.multiple_of(start, BALL), BALL), :].astype(BF16)

    def their_ball(ball, carry):
        theirs_rows[here(ball), :] = pick_rows(other_c * HALF + ball * BALL)
        points_copy(ball).start()
        return carry

    theirs_rows[0:BALL, :] = pick_rows(other_c * HALF)
    own_small = jnp.concatenate([gain_ref[...], tree_gain_ref[...], jnp.zeros((3, LOCAL), F32)], axis=0)
    sm[pl.ds(c, 1)] = own_small[None]
    pl.semaphore_wait(barrier, 45)
    small_copy().start()
    points_copy(0).start()
    lax.fori_loop(1, BALLS, their_ball, 0)

    early_rows = pl.ds(pl.multiple_of(local_range * 16, 16), 16)
    sums = [
        jnp.sum(cot[ball * BALL:(ball + 1) * BALL, :].astype(F32), axis=0, keepdims=True)
        for ball in range(ROWS // BALL)
    ]
    early[early_rows, 0:LOCAL] = jnp.concatenate(sums, axis=0)
    early[early_rows, LOCAL:] = jnp.concatenate(
        [slots[...].astype(F32), jnp.zeros((16, LOCAL - LEVELS), F32)], axis=1
    )

    def early_copy(distance):
        block = early.at[early_rows]
        return send(block, block, s_early, distance, early_peer(distance))

    for distance in range(1, GROUP):
        early_copy(distance).start()

    cth[pl.ds(c, 1)] = cot[pl.ds(pl.multiple_of(c * HALF, HALF), HALF), :][None]
    for index in range(3):
        wt[index] = jnp.transpose(w[index])
        wcat[:, index * WIDTH:(index + 1) * WIDTH] = w[index]

    def own_ball(ball, carry):
        xh[pl.ds(c, 1), here(ball), :] = pick_rows(c * HALF + ball * BALL)[None]
        return carry

    lax.fori_loop(0, BALLS, own_ball, 0)
    small_copy().wait_recv()
    gain = jnp.concatenate([sm[0, 0:1, :], sm[1, 0:1, :]], axis=1)
    bands = [slice(head * HEAD, (head + 1) * HEAD) for head in range(HEADS)]

    def forward(ball, carry):
        rows = here(ball)
        points_copy(ball).wait_recv()

        @pl.when(ball < EARLY_COT)
        def _():
            cot_copy(ball).start()

        ordered = both(xh, rows)
        mean = jnp.sum(ordered * ordered, axis=1, keepdims=True) * (1.0 / WIDTH)
        inverse = lax.rsqrt(mean + EPSILON)
        normed = (ordered * inverse * gain).astype(BF16)
        keyset = nn(normed, w[1]).astype(BF16)
        query_t = nt(wt[0], normed).astype(BF16)
        value_t = nt(wt[2], normed).astype(BF16)
        scores = [nn(keyset[:, band], query_t[band, :]) for band in bands]
        key_t = nt(wt[1], normed).astype(BF16)
        value = nn(normed, w[2]).astype(BF16)
        halves = []
        for head in range(HEADS):
            top = jnp.max(scores[head], axis=0, keepdims=True)
            weights = jnp.exp2((scores[head] - top) * SCALE_LOG2)
            scaled = weights * (1.0 / jnp.sum(weights, axis=0, keepdims=True))
            probs[ball * HEADS + head] = scaled
            halves.append(scaled.astype(BF16))
        attended_t = jnp.concatenate(
            [nn(value_t[band, :], half).astype(BF16) for band, half in zip(bands, halves)], axis=0
        )
        projected = nn(jnp.transpose(attended_t), wo[...])
        hidden = ordered + projected
        node = jnp.sum(hidden, axis=0, keepdims=True) * BALL ** (-0.5)
        nodes_own[0, pl.ds(ball, 1), :] = node[:, :LOCAL]
        nodes_own[1, pl.ds(ball, 1), :] = node[:, LOCAL:]
        hid[0, rows, :] = hidden[:, :LOCAL]
        hid[1, rows, :] = hidden[:, LOCAL:]
        pstage[0, rows, :] = projected[:, :LOCAL].astype(BF16)
        pstage[1, rows, :] = projected[:, LOCAL:].astype(BF16)
        inv[rows, :] = jnp.broadcast_to(inverse, (BALL, LOCAL))
        nrm[rows, :] = normed
        vn[rows, :] = value
        q_t[ball] = query_t
        k_t[ball] = key_t
        att_t[ball] = attended_t
        return carry

    lax.fori_loop(0, BALLS, forward, 0)

    node_rows = pl.ds(pl.multiple_of(me * BALLS, BALLS), BALLS)

    def tree_copy(distance):
        return send(
            nodes_own.at[(me + distance) % 2], nodes.at[node_rows], s_tree, distance, tree_peer(distance)
        )

    for distance in range(1, 32):
        tree_copy(distance).start()
    for ball in range(EARLY_COT, BALLS):
        cot_copy(ball).start()
    nodes[node_rows, :] = nodes_own[pl.ds(c, 1)][0]

    for distance in range(1, GROUP):
        early_copy(distance).wait_recv()
    count = GROUP * 16
    range_ids = lax.broadcasted_iota(jnp.int32, (count, 1), 0) // 16
    lane_ids = lax.broadcasted_iota(jnp.int32, (count, count), 1)
    for level in range(LEVELS):
        slot = early[:, LOCAL + level:LOCAL + level + 1].astype(jnp.int32)
        bit = (range_ids // (1 << level)) % 2
        partner = (range_ids + (1 - 2 * bit) * (1 << level)) * 16 + slot
        onehot = jnp.where(lane_ids == partner, 1.0, 0.0).astype(BF16)
        picks[level] = onehot
        picks_t[level] = jnp.transpose(onehot)
    acc_t[...] = jnp.zeros_like(acc_t)
    own_gains = sm[pl.ds(c, 1)][0]

    for distance in range(1, 32):
        tree_copy(distance).wait_recv()
    states = nodes[...]
    chosen_list = []
    for level in range(LEVELS):
        chosen = exact_dot(picks[level], states)
        states = states + own_gains[1 + level:2 + level, :] * (chosen * jax.nn.sigmoid(chosen))
        chosen_list.append(chosen)
    node_grad = early[:, 0:LOCAL]
    for level in reversed(range(LEVELS)):
        chosen = chosen_list[level]
        sigma = jax.nn.sigmoid(chosen)
        slope = sigma * (1.0 + chosen * (1.0 - sigma))
        node_grad = node_grad + exact_dot(
            picks_t[level], own_gains[1 + level:2 + level, :] * slope * node_grad
        )
    final_grad[...] = node_grad
    final_state[...] = states

    def range_row(half, ball):
        return local_range * 16 + half * BALLS + ball

    def ng_copy():
        part = final_grad.at[pl.ds(pl.multiple_of(range_row(other_c, 0), BALLS), BALLS)]
        return send(part, node_grads.at[c], s_ng, 0, pair)

    ng_copy().start()
    for ball in range(BALLS):
        proj_copy(ball).start()
    node_grads[pl.ds(c, 1)] = final_grad[pl.ds(pl.multiple_of(range_row(c, 0), BALLS), BALLS), :][None]

    def own_mixed(ball, carry):
        state = final_state[pl.ds(range_row(c, ball), 1), :]
        mixed[ours(ball), :] = (hid[pl.ds(c, 1), here(ball), :][0] + state).astype(BF16)
        return carry

    lax.fori_loop(0, BALLS, own_mixed, 0)
    ng_copy().wait_recv()

    def backward(ball, carry):
        rows = here(ball)
        cot_copy(ball).wait_recv()
        shift = jnp.concatenate(
            [node_grads[0, pl.ds(ball, 1), :], node_grads[1, pl.ds(ball, 1), :]], axis=1
        ) * BALL ** (-0.5)
        hidden_grad = (both(cth, rows) + shift).astype(BF16)
        att_grad = nt(wo[...], hidden_grad).astype(BF16)
        value = vn[rows, :]
        prob_grads = [nn(value[:, band], att_grad[band, :]) for band in bands]
        acc_t[768:1024, :] += nn(att_t[ball], hidden_grad)
        score_grads, halves = [], []
        for head in range(HEADS):
            prob = probs[ball * HEADS + head]
            dots = jnp.sum(prob_grads[head] * prob, axis=0, keepdims=True)
            score_grads.append((prob * (prob_grads[head] - dots) * SCALE).astype(BF16))
            halves.append(prob.astype(BF16))
        dv = [nt(att_grad[band, :], half).astype(BF16) for band, half in zip(bands, halves)]
        key_t = k_t[ball]
        dq = [nn(key_t[band, :], part).astype(BF16) for band, part in zip(bands, score_grads)]
        query_t = q_t[ball]
        dk = [nt(query_t[band, :], part).astype(BF16) for band, part in zip(bands, score_grads)]
        all_grads = jnp.concatenate(dq + dk + dv, axis=0)
        normed_grad = nn(wcat[...], all_grads)
        acc_t[0:768, :] += nn(all_grads, nrm[rows, :])
        scaled_grad = jnp.transpose(normed_grad) * gain
        ordered = both(xh, rows)
        inverse = jnp.concatenate([inv[rows, :], inv[rows, :]], axis=1)
        correction = jnp.sum(ordered * scaled_grad, axis=1, keepdims=True) * (1.0 / WIDTH)
        ordered_grad = (
            hidden_grad.astype(F32) + inverse * scaled_grad - ordered * (inverse * inverse * inverse) * correction
        ).astype(BF16)
        gstage[0, rows, :] = ordered_grad[:, :LOCAL]
        gstage[1, rows, :] = ordered_grad[:, LOCAL:]
        grad_copy(ball).start()
        grads[ours(ball), :] = gstage[pl.ds(c, 1), rows, :][0]
        return carry

    lax.fori_loop(0, BALLS, backward, 0)

    for index in range(3):
        part = jnp.transpose(acc_t[index * 256:(index + 1) * 256, :])
        acc[0, index * 256:(index + 1) * 256, :] = part[:, :LOCAL]
        acc[1, index * 256:(index + 1) * 256, :] = part[:, LOCAL:]
    for half in range(2):
        band = slice(768 + half * LOCAL, 768 + (half + 1) * LOCAL)
        acc[half, 768:896, :] = acc_t[band, :LOCAL]
        acc[half, 896:1024, :] = acc_t[band, LOCAL:]

    kept = pl.ds(pl.multiple_of(core * 512, 512), 512)
    given = pl.ds(pl.multiple_of((1 - core) * 512, 512), 512)
    copy_a = send(acc.at[:, given], recv_a, s_a, 0, sibling)
    copy_a.start()

    def their_mixed(ball, carry):
        rows = here(ball)
        proj_copy(ball).wait_recv()
        state = final_state[pl.ds(range_row(other_c, ball), 1), :]
        mixed[theirs(ball), :] = (
            theirs_rows[rows, :].astype(F32) + precv[rows, :].astype(F32) + state
        ).astype(BF16)
        return carry

    copy_a.wait_recv()
    sum_a[...] = acc[:, kept, :] + recv_a[...]

    def copy_c(distance):
        piece = pl.ds(pl.multiple_of(plane_index(distance) * 32, 32), 32)
        return send(sum_a.at[:, piece], recv_c.at[distance], s_c, distance, plane_peer(distance))

    for distance in range(1, 16):
        copy_c(distance).start()
    lax.fori_loop(0, BALLS, their_mixed, 0)
    part = sum_a[:, pl.ds(pl.multiple_of(plane * 32, 32), 32), :]
    for distance in range(1, 16):
        copy_c(distance).wait_recv()
        part = part + recv_c[distance]
    sum_c[...] = part

    def copy_z(distance):
        return send(sum_c.at[(ring + distance) % 2], recv_z.at[ring], s_z, distance, ring_peer(distance))

    for distance in range(1, 8):
        copy_z(distance).start()
    recv_z[pl.ds(ring, 1)] = sum_c[pl.ds(c, 1)]
    for distance in range(1, 8):
        copy_z(distance).wait_recv()
    part = recv_z[0]
    for step in range(1, 8):
        part = part + recv_z[step]
    plane_rows = pl.ds(pl.multiple_of(plane * 32, 32), 32)
    all_f[plane_rows, :] = part

    def copy_f(distance):
        return send(all_f.at[plane_rows], all_f.at[plane_rows], s_f, distance, plane_peer(distance))

    for distance in range(1, 16):
        copy_f(distance).start()
    for distance in range(1, 16):
        copy_f(distance).wait_recv()

    copy_g = send(all_f, total.at[kept], s_g, 0, sibling)
    copy_g.start()
    total[kept, :] = all_f[...]
    copy_g.wait_recv()
    for index in range(3):
        qkv_out[index] = total[index * 256:(index + 1) * 256, :]
    out_out[:, :LOCAL] = total[768:896, :]
    out_out[:, LOCAL:] = total[896:1024, :]

    small_copy().wait_send()
    ng_copy().wait_send()

    def settle(ball, carry):
        points_copy(ball).wait_send()
        cot_copy(ball).wait_send()
        proj_copy(ball).wait_send()
        grad_copy(ball).wait()
        return carry

    lax.fori_loop(0, BALLS, settle, 0)
    for distance in range(1, 32):
        tree_copy(distance).wait_send()
    copy_a.wait_send()
    for distance in range(1, 16):
        early_copy(distance).wait_send()
        copy_c(distance).wait_send()
        copy_f(distance).wait_send()
    for distance in range(1, 8):
        copy_z(distance).wait_send()
    copy_g.wait_send()


def run_main(order, points, cot, gain, tree_gain, slots, w, wo):
    vmem = pl.BlockSpec(memory_space=pltpu.VMEM)
    sems = lambda count: pltpu.SemaphoreType.DMA((2, count))
    v = pltpu.VMEM
    return pl.pallas_call(
        main_kernel,
        out_shape=(
            jax.ShapeDtypeStruct((ROWS, LOCAL), BF16),
            jax.ShapeDtypeStruct((ROWS, LOCAL), BF16),
            jax.ShapeDtypeStruct((3, WIDTH, LOCAL), F32),
            jax.ShapeDtypeStruct((LOCAL, WIDTH), F32),
        ),
        in_specs=[pl.BlockSpec(memory_space=pltpu.SMEM)] + [vmem] * 7,
        out_specs=(vmem,) * 4,
        scratch_shapes=[
            v((ROWS, LOCAL), F32),
            v((ROWS, LOCAL), F32),
            v((HALF, LOCAL), BF16),
            v((2, HALF, LOCAL), BF16),
            v((2, HALF, LOCAL), BF16),
            v((2, 8, LOCAL), F32),
            v((3, WIDTH, WIDTH), BF16),
            v((WIDTH, 3 * WIDTH), BF16),
            v((HALF, WIDTH), BF16),
            v((BALLS, WIDTH, BALL), BF16),
            v((BALLS, WIDTH, BALL), BF16),
            v((BALLS, WIDTH, BALL), BF16),
            v((HALF, WIDTH), BF16),
            v((2, HALF, LOCAL), F32),
            v((HALF, LOCAL), F32),
            v((BALLS * HEADS, BALL, BALL), F32),
            v((256, 2 * LOCAL), F32),
            v((2, BALLS, LOCAL), F32),
            v((256, LOCAL), F32),
            v((LEVELS, 256, 256), BF16),
            v((LEVELS, 256, 256), BF16),
            v((256, LOCAL), F32),
            v((256, LOCAL), F32),
            v((2, BALLS, LOCAL), F32),
            v((2, HALF, LOCAL), BF16),
            v((HALF, LOCAL), BF16),
            v((2, HALF, LOCAL), BF16),
            v((1024, WIDTH), F32),
            v((2, 1024, LOCAL), F32),
            v((2, 512, LOCAL), F32),
            v((2, 512, LOCAL), F32),
            v((16, 2, 32, LOCAL), F32),
            v((2, 32, LOCAL), F32),
            v((8, 32, LOCAL), F32),
            v((512, LOCAL), F32),
            v((1024, LOCAL), F32),
            sems(1), sems(BALLS), sems(BALLS), sems(BALLS), sems(BALLS), sems(16), sems(32),
            sems(1), sems(1), sems(16), sems(8), sems(16), sems(1),
        ],
        compiler_params=pltpu.CompilerParams(
            collective_id=0, has_side_effects=True, vmem_limit_bytes=58 * 1024 * 1024
        ),
        cost_estimate=pl.CostEstimate(flops=8 * 10**9, bytes_accessed=8 * 10**6, transcendentals=4 * 10**6),
    )(order, points, cot, gain, tree_gain, slots, w, wo)


def local(points, order, norm_gain, qkv_weight, out_weight, tree_gain, partner_slot, cotangent):
    mixed, grads, qkv_total, out_total = run_main(
        order, points, cotangent, norm_gain[None], tree_gain, partner_slot, qkv_weight, out_weight
    )
    point_grad = permute_rows(scatter_kernel, order, grads)
    return (mixed, point_grad, qkv_total, out_total)


def solution(mesh):
    in_specs = (
        P("pts", "ch"),
        P("pts"),
        P("ch"),
        P(),
        P(),
        P(None, "ch"),
        P("pts", None),
        P("pts", "ch"),
    )
    out_specs = (P("pts", "ch"), P("pts", "ch"), P(None, None, "ch"), P("ch", None))
    return jax.shard_map(local, mesh=mesh, in_specs=in_specs, out_specs=out_specs, check_vma=False)
```

time: 131 us -> 96.9 us (0.74)
  Pallas kernels: 121 us -> 90.5 us
  local copies, waits for them, and re-layouts: 7.94 us -> 5.49 us
  other arithmetic: 1.33 us -> 0 us
    pallas_call x1, Pallas kernels: 109 us -> 84.1 us  [run_main(): pl.pallas_call(main_kernel, out_shape=(jax.ShapeDtypeStruct((ROWS, LOCAL)...]
    pallas_call x2 -> x1, Pallas kernels: 11.8 us -> 6.45 us  [permute_rows(): pl.pallas_call(kernel, out_shape=jax.ShapeDtypeStruct((ROWS, LOCAL), BF16...]
    slice x2 -> x0, local copies, waits for them, and re-layouts: 2.74 us -> none  [the longest x1 1.77 us: local(): qkv_total = total[:768].reshape(3, WIDTH, LOCAL)]
    concatenate x2 -> x0, other arithmetic: 1.33 us -> none  [the longest x1 0.66 us: local(): out_total = jnp.concatenate([total[768:896], total[896:]], axis=1)]
    unnamed x17 -> x14, local copies, waits for them, and re-layouts: 4.44 us -> 5.49 us
where the time goes in v2:
time: 96.9 us; the launch traced here: 96.7 us
  Pallas kernels  90.5 us (93%)
  local copies, waits for them, and re-layouts  5.49 us (6%)
    pallas_call x1, Pallas kernels, run_main(): pl.pallas_call(main_kernel, out_shape=(jax.ShapeDtypeStruct((ROWS, LOCAL)...  84.1 us
    pallas_call x1, Pallas kernels, permute_rows(): pl.pallas_call(kernel, out_shape=jax.ShapeDtypeStruct((ROWS, LOCAL), BF16...  6.45 us
    unnamed x14, local copies, waits for them, and re-layouts  5.49 us

profile of v2, /device:TPU:1, one launch (start us, length us, event | category | flops | bytes accessed | tf_op | source)
XLA Modules:
  0.0 96.7 jit_solution(11226980576925262143)
XLA Ops:
  0.6 1.4 %copy.12.slots = s32[16,4]{1,0:T(8,128)} copy(s32[16,4]{0,1:T(4,128)} %param.14) | data formatting | bytes 512 | tf_op args[6]
  2.0 0.0 copy-start.1
  2.0 84.1 %shard_map.111 = (bf16[4096,128]{1,0:T(8,128)(2,1)}, bf16[4096,128]{1,0:T(8,128)(2,1)}, f32[3,256,128]{2,1,0:T(8,128)}, f32[128,256]{1,0:T(8,128)}) custom-call(s32[4096]{0:T(1024)} %order_ref.3, bf16[4096,128]{1,0:T(8,128)(2,1)} %points.1, bf16[4096,128]{1,0:T(8,128)(2,1)} %cot.1, f32[1,128]{1,0:T(1,128)} %bitcast.1, f32[4,128]{1,0:T(4,128)} %tree_gain_ref.1, ...), custom_call_target="tpu_custom_call" | custom-call | flops 8000000000 | bytes 8000000 | tf_op jit(solution)/shard_map/pallas_call | solution.py:467
  86.1 0.0 copy-done.1
  86.1 0.0 copy-start
  86.1 1.2 %copy-done = bf16[4096,128]{1,0:T(8,128)(2,1)S(1)} copy-done((bf16[4096,128]{1,0:T(8,128)(2,1)S(1)}, bf16[4096,128]{1,0:T(8,128)(2,1)}, u32[]{:S(2)}) %copy-start) | copy-done | bytes 1048600
  87.3 0.0 copy-start.2
  87.3 6.5 %shard_map.112 = bf16[4096,128]{1,0:T(8,128)(2,1)} custom-call(s32[4096]{0:T(1024)S(1)} %copy-done.1, bf16[4096,128]{1,0:T(8,128)(2,1)S(1)} %copy-done), custom_call_target="tpu_custom_call" | custom-call | tf_op jit(solution)/shard_map/pallas_call | solution.py:54
  93.7 0.0 copy-done.2
  93.7 0.0 copy-start.3
  93.8 1.0 %copy.16 = bf16[4096,128]{1,0:T(8,128)(2,1)} copy(bf16[4096,128]{1,0:T(8,128)(2,1)S(1)} %copy-done.2) | data formatting | bytes 2097152
  94.7 0.3 copy-done.3
  95.0 0.0 copy-start.4
  95.0 0.7 copy.17
  95.7 0.3 copy-done.4
  96.0 0.7 copy.18
Async XLA Ops:
  2.0 84.1 %copy-start.1 = (s32[4096]{0:T(1024)S(1)}, s32[4096]{0:T(1024)}, u32[]{:S(2)}) copy-start(s32[4096]{0:T(1024)} %order_ref.3) | copy-start | bytes 49156
  86.1 1.2 %copy-start = (bf16[4096,128]{1,0:T(8,128)(2,1)S(1)}, bf16[4096,128]{1,0:T(8,128)(2,1)}, u32[]{:S(2)}) copy-start(bf16[4096,128]{1,0:T(8,128)(2,1)} %get-tuple-element.9.rows_ref) | copy-start | bytes 3145732
  87.3 6.5 %copy-start.2 = (bf16[4096,128]{1,0:T(8,128)(2,1)S(1)}, bf16[4096,128]{1,0:T(8,128)(2,1)}, u32[]{:S(2)}) copy-start(bf16[4096,128]{1,0:T(8,128)(2,1)} %get-tuple-element.16) | copy-start | bytes 3145732
  93.7 1.2 %copy-start.3 = (f32[3,256,128]{2,1,0:T(8,128)S(1)}, f32[3,256,128]{2,1,0:T(8,128)}, u32[]{:S(2)}) copy-start(f32[3,256,128]{2,1,0:T(8,128)} %get-tuple-element.18) | copy-start | bytes 1179652
  95.0 1.0 %copy-start.4 = (f32[128,256]{1,0:T(8,128)S(1)}, f32[128,256]{1,0:T(8,128)}, u32[]{:S(2)}) copy-start(f32[128,256]{1,0:T(8,128)} %get-tuple-element.19) | copy-start | bytes 393220

commit v3 on v2

--- a/solution.py
+++ b/solution.py
@@ -36,31 +36,6 @@
     return lax.dot_general(left, right, (((1,), (1,)), ((), ())), preferred_element_type=F32)
 
 
-def scatter_kernel(order_ref, rows_ref, out_ref, wide, moved):
-    wide[...] = rows_ref[...].astype(F32)
-
-    def step(block, carry):
-        base = block * 16
-        for inner in range(16):
-            row = order_ref[base + inner]
-            moved[pl.ds(row, 1), :] = wide[pl.ds(base + inner, 1), :]
-        return carry
-
-    lax.fori_loop(0, ROWS // 16, step, 0)
-    out_ref[...] = moved[...].astype(BF16)
-
-
-def permute_rows(kernel, order, rows):
-    return pl.pallas_call(
-        kernel,
-        out_shape=jax.ShapeDtypeStruct((ROWS, LOCAL), BF16),
-        in_specs=[pl.BlockSpec(memory_space=pltpu.SMEM), pl.BlockSpec(memory_space=pltpu.VMEM)],
-        out_specs=pl.BlockSpec(memory_space=pltpu.VMEM),
-        scratch_shapes=[pltpu.VMEM((ROWS, LOCAL), F32), pltpu.VMEM((ROWS, LOCAL), F32)],
-        compiler_params=pltpu.CompilerParams(vmem_limit_bytes=24 * 1024 * 1024),
-    )(order, rows)
-
-
 def exact_dot(onehot, values):
     high = values.astype(BF16)
     rest = values - high.astype(F32)
@@ -71,12 +46,13 @@
 
 
 def main_kernel(
-    order_ref, points, cot, gain_ref, tree_gain_ref, slots, w, wo,
-    mixed, grads, qkv_out, out_out,
+    order_ref, order_rows, points, cot, gain_ref, tree_gain_ref, slots_t, w, wo,
+    mixed, point_grad, qkv_out, out_out,
     wide, moved, theirs_rows, xh, cth, sm, wt, wcat, vn, q_t, k_t, att_t, nrm, hid, inv, probs,
-    early, nodes_own, nodes, picks, picks_t, final_state, final_grad, node_grads,
+    early, chip_nodes, nodes, picks, picks_t, final_state, final_grad, node_grads,
     pstage, precv, gstage, acc_t,
-    acc, recv_a, sum_a, recv_c, sum_c, recv_z, all_f, total,
+    acc, recv_a, sum_a, half_a, recv_c, sum_c, recv_z, all_f, total,
+    grads, places, places_smem, s_places,
     s_small, s_pts, s_cot, s_proj, s_grad, s_early, s_tree, s_ng, s_a, s_c, s_z, s_f, s_g,
 ):
     p = lax.axis_index("pts")
@@ -86,18 +62,18 @@
     depth = p // 32
     other_c = 1 - c
     local_range = p % GROUP
-    me = local_range * 2 + c
+    chip = local_range // 2
     group_base = (p // GROUP) * GROUP
     ring = depth * 2 + c
     pair = (p, other_c)
     sibling = (p + 1 - 2 * core, c)
 
     def tree_peer(distance):
-        there = (me + distance) % 32
-        return (group_base + there // 2, there % 2)
+        there = (chip * 2 + c + distance) % 16
+        return (group_base + (there // 2) * 2 + core, there % 2)
 
     def early_peer(distance):
-        return (group_base + (local_range + distance) % GROUP, c)
+        return (group_base + ((chip + distance) % 8) * 2 + core, c)
 
     def plane_index(distance):
         return (plane + distance) % 16
@@ -114,7 +90,8 @@
     def greet(target):
         pl.semaphore_signal(barrier, inc=1, device_id=target, device_id_type=MESH)
 
-    for distance in range(1, 32):
+    greet(sibling)
+    for distance in range(1, 16):
         greet(tree_peer(distance))
     far_base = (1 - plane // 8) * 8
     for step in range(8):
@@ -177,27 +154,39 @@
     theirs_rows[0:BALL, :] = pick_rows(other_c * HALF)
     own_small = jnp.concatenate([gain_ref[...], tree_gain_ref[...], jnp.zeros((3, LOCAL), F32)], axis=0)
     sm[pl.ds(c, 1)] = own_small[None]
-    pl.semaphore_wait(barrier, 45)
+    pl.semaphore_wait(barrier, 30)
     small_copy().start()
     points_copy(0).start()
     lax.fori_loop(1, BALLS, their_ball, 0)
 
-    early_rows = pl.ds(pl.multiple_of(local_range * 16, 16), 16)
-    sums = [
-        jnp.sum(cot[ball * BALL:(ball + 1) * BALL, :].astype(F32), axis=0, keepdims=True)
-        for ball in range(ROWS // BALL)
-    ]
-    early[early_rows, 0:LOCAL] = jnp.concatenate(sums, axis=0)
-    early[early_rows, LOCAL:] = jnp.concatenate(
-        [slots[...].astype(F32), jnp.zeros((16, LOCAL - LEVELS), F32)], axis=1
+    slots = jnp.transpose(
+        jnp.concatenate(
+            [
+                jnp.concatenate([slots_t[...].astype(F32), jnp.zeros((LEVELS, LOCAL - 16), F32)], axis=1),
+                jnp.zeros((LOCAL - LEVELS, LOCAL), F32),
+            ],
+            axis=0,
+        )
     )
+    range_rows = pl.ds(pl.multiple_of(local_range * BALLS, BALLS), BALLS)
+    chip_rows = pl.ds(pl.multiple_of(chip * 16, 16), 16)
+    for half in range(2):
+        sums = [
+            jnp.sum(cot[ball * BALL:(ball + 1) * BALL, :].astype(F32), axis=0, keepdims=True)
+            for ball in range(half * BALLS, (half + 1) * BALLS)
+        ]
+        early[half, range_rows, 0:LOCAL] = jnp.concatenate(sums, axis=0)
+        early[half, range_rows, LOCAL:] = slots[half * BALLS:(half + 1) * BALLS, :]
+
+    def early_first():
+        block = early.at[:, range_rows]
+        return send(block, block, s_early, 0, sibling)
 
     def early_copy(distance):
-        block = early.at[early_rows]
+        block = early.at[:, chip_rows]
         return send(block, block, s_early, distance, early_peer(distance))
 
-    for distance in range(1, GROUP):
-        early_copy(distance).start()
+    early_first().start()
 
     cth[pl.ds(c, 1)] = cot[pl.ds(pl.multiple_of(c * HALF, HALF), HALF), :][None]
     for index in range(3):
@@ -209,17 +198,28 @@
         return carry
 
     lax.fori_loop(0, BALLS, own_ball, 0)
+    early_first().wait_recv()
+    for distance in range(1, 8):
+        early_copy(distance).start()
     small_copy().wait_recv()
     gain = jnp.concatenate([sm[0, 0:1, :], sm[1, 0:1, :]], axis=1)
     bands = [slice(head * HEAD, (head + 1) * HEAD) for head in range(HEADS)]
 
-    def forward(ball, carry):
-        rows = here(ball)
-        points_copy(ball).wait_recv()
-
-        @pl.when(ball < EARLY_COT)
+    def two(step):
+        return pl.ds(pl.multiple_of(step * 2 * BALL, 2 * BALL), 2 * BALL)
+
+    pieces = [(side, band) for side in range(2) for band in bands]
+    sides = [slice(0, BALL), slice(BALL, 2 * BALL)]
+
+    def forward(step, carry):
+        rows = two(step)
+        for side in range(2):
+            points_copy(2 * step + side).wait_recv()
+
+        @pl.when(step < EARLY_COT // 2)
         def _():
-            cot_copy(ball).start()
+            for side in range(2):
+                cot_copy(2 * step + side).start()
 
         ordered = both(xh, rows)
         mean = jnp.sum(ordered * ordered, axis=1, keepdims=True) * (1.0 / WIDTH)
@@ -228,75 +228,87 @@
         keyset = nn(normed, w[1]).astype(BF16)
         query_t = nt(wt[0], normed).astype(BF16)
         value_t = nt(wt[2], normed).astype(BF16)
-        scores = [nn(keyset[:, band], query_t[band, :]) for band in bands]
+        scores = [nn(keyset[sides[side], band], query_t[band, sides[side]]) for side, band in pieces]
         key_t = nt(wt[1], normed).astype(BF16)
         value = nn(normed, w[2]).astype(BF16)
         halves = []
-        for head in range(HEADS):
-            top = jnp.max(scores[head], axis=0, keepdims=True)
-            weights = jnp.exp2((scores[head] - top) * SCALE_LOG2)
+        for index in range(2 * HEADS):
+            top = jnp.max(scores[index], axis=0, keepdims=True)
+            weights = jnp.exp2((scores[index] - top) * SCALE_LOG2)
             scaled = weights * (1.0 / jnp.sum(weights, axis=0, keepdims=True))
-            probs[ball * HEADS + head] = scaled
+            probs[step * 2 * HEADS + index] = scaled
             halves.append(scaled.astype(BF16))
+        parts = [
+            nn(value_t[band, sides[side]], half).astype(BF16) for (side, band), half in zip(pieces, halves)
+        ]
         attended_t = jnp.concatenate(
-            [nn(value_t[band, :], half).astype(BF16) for band, half in zip(bands, halves)], axis=0
+            [jnp.concatenate(parts[:HEADS], axis=0), jnp.concatenate(parts[HEADS:], axis=0)], axis=1
         )
         projected = nn(jnp.transpose(attended_t), wo[...])
         hidden = ordered + projected
-        node = jnp.sum(hidden, axis=0, keepdims=True) * BALL ** (-0.5)
-        nodes_own[0, pl.ds(ball, 1), :] = node[:, :LOCAL]
-        nodes_own[1, pl.ds(ball, 1), :] = node[:, LOCAL:]
+        for side in range(2):
+            node = jnp.sum(hidden[sides[side], :], axis=0, keepdims=True) * BALL ** (-0.5)
+            row = pl.ds(core * BALLS + 2 * step + side, 1)
+            chip_nodes[0, row, :] = node[:, :LOCAL]
+            chip_nodes[1, row, :] = node[:, LOCAL:]
+            q_t[2 * step + side] = query_t[:, sides[side]]
+            k_t[2 * step + side] = key_t[:, sides[side]]
         hid[0, rows, :] = hidden[:, :LOCAL]
         hid[1, rows, :] = hidden[:, LOCAL:]
         pstage[0, rows, :] = projected[:, :LOCAL].astype(BF16)
         pstage[1, rows, :] = projected[:, LOCAL:].astype(BF16)
-        inv[rows, :] = jnp.broadcast_to(inverse, (BALL, LOCAL))
+        inv[rows, :] = jnp.broadcast_to(inverse, (2 * BALL, LOCAL))
         nrm[rows, :] = normed
         vn[rows, :] = value
-        q_t[ball] = query_t
-        k_t[ball] = key_t
-        att_t[ball] = attended_t
+        att_t[step] = attended_t
         return carry
 
-    lax.fori_loop(0, BALLS, forward, 0)
-
-    node_rows = pl.ds(pl.multiple_of(me * BALLS, BALLS), BALLS)
+    lax.fori_loop(0, BALLS // 2, forward, 0)
+
+    core_rows = pl.ds(pl.multiple_of(core * BALLS, BALLS), BALLS)
+
+    def tree_first():
+        block = chip_nodes.at[:, core_rows]
+        return send(block, block, s_tree, 0, sibling)
 
     def tree_copy(distance):
         return send(
-            nodes_own.at[(me + distance) % 2], nodes.at[node_rows], s_tree, distance, tree_peer(distance)
+            chip_nodes.at[(c + distance) % 2], nodes.at[c, chip_rows], s_tree, distance, tree_peer(distance)
         )
 
-    for distance in range(1, 32):
+    tree_first().start()
+    tree_first().wait_recv()
+    for distance in range(1, 16):
         tree_copy(distance).start()
     for ball in range(EARLY_COT, BALLS):
         cot_copy(ball).start()
-    nodes[node_rows, :] = nodes_own[pl.ds(c, 1)][0]
-
-    for distance in range(1, GROUP):
+    nodes[pl.ds(c, 1), chip_rows, :] = chip_nodes[pl.ds(c, 1)]
+
+    for distance in range(1, 8):
         early_copy(distance).wait_recv()
     count = GROUP * 16
-    range_ids = lax.broadcasted_iota(jnp.int32, (count, 1), 0) // 16
+    range_ids = (lax.broadcasted_iota(jnp.int32, (count, 1), 0) % LOCAL) // BALLS
     lane_ids = lax.broadcasted_iota(jnp.int32, (count, count), 1)
+    known = jnp.concatenate([early[0], early[1]], axis=0)
     for level in range(LEVELS):
-        slot = early[:, LOCAL + level:LOCAL + level + 1].astype(jnp.int32)
+        slot = known[:, LOCAL + level:LOCAL + level + 1].astype(jnp.int32)
         bit = (range_ids // (1 << level)) % 2
-        partner = (range_ids + (1 - 2 * bit) * (1 << level)) * 16 + slot
+        partner = (slot // BALLS) * LOCAL + (range_ids + (1 - 2 * bit) * (1 << level)) * BALLS + slot % BALLS
         onehot = jnp.where(lane_ids == partner, 1.0, 0.0).astype(BF16)
         picks[level] = onehot
         picks_t[level] = jnp.transpose(onehot)
     acc_t[...] = jnp.zeros_like(acc_t)
     own_gains = sm[pl.ds(c, 1)][0]
 
-    for distance in range(1, 32):
+    for distance in range(1, 16):
         tree_copy(distance).wait_recv()
-    states = nodes[...]
+    states = jnp.concatenate([nodes[0], nodes[1]], axis=0)
     chosen_list = []
     for level in range(LEVELS):
         chosen = exact_dot(picks[level], states)
         states = states + own_gains[1 + level:2 + level, :] * (chosen * jax.nn.sigmoid(chosen))
         chosen_list.append(chosen)
-    node_grad = early[:, 0:LOCAL]
+    node_grad = known[:, 0:LOCAL]
     for level in reversed(range(LEVELS)):
         chosen = chosen_list[level]
         sigma = jax.nn.sigmoid(chosen)
@@ -308,7 +320,7 @@
     final_state[...] = states
 
     def range_row(half, ball):
-        return local_range * 16 + half * BALLS + ball
+        return half * LOCAL + local_range * BALLS + ball
 
     def ng_copy():
         part = final_grad.at[pl.ds(pl.multiple_of(range_row(other_c, 0), BALLS), BALLS)]
@@ -327,29 +339,43 @@
     lax.fori_loop(0, BALLS, own_mixed, 0)
     ng_copy().wait_recv()
 
-    def backward(ball, carry):
-        rows = here(ball)
-        cot_copy(ball).wait_recv()
-        shift = jnp.concatenate(
-            [node_grads[0, pl.ds(ball, 1), :], node_grads[1, pl.ds(ball, 1), :]], axis=1
-        ) * BALL ** (-0.5)
-        hidden_grad = (both(cth, rows) + shift).astype(BF16)
+    def backward(step, carry):
+        rows = two(step)
+        shifts = []
+        for side in range(2):
+            cot_copy(2 * step + side).wait_recv()
+            row = pl.ds(2 * step + side, 1)
+            shift = jnp.concatenate([node_grads[0, row, :], node_grads[1, row, :]], axis=1) * BALL ** (-0.5)
+            shifts.append(jnp.broadcast_to(shift, (BALL, WIDTH)))
+        hidden_grad = (both(cth, rows) + jnp.concatenate(shifts, axis=0)).astype(BF16)
         att_grad = nt(wo[...], hidden_grad).astype(BF16)
         value = vn[rows, :]
-        prob_grads = [nn(value[:, band], att_grad[band, :]) for band in bands]
-        acc_t[768:1024, :] += nn(att_t[ball], hidden_grad)
+        prob_grads = [nn(value[sides[side], band], att_grad[band, sides[side]]) for side, band in pieces]
+        acc_t[768:1024, :] += nn(att_t[step], hidden_grad)
         score_grads, halves = [], []
-        for head in range(HEADS):
-            prob = probs[ball * HEADS + head]
-            dots = jnp.sum(prob_grads[head] * prob, axis=0, keepdims=True)
-            score_grads.append((prob * (prob_grads[head] - dots) * SCALE).astype(BF16))
+        for index in range(2 * HEADS):
+            prob = probs[step * 2 * HEADS + index]
+            dots = jnp.sum(prob_grads[index] * prob, axis=0, keepdims=True)
+            score_grads.append((prob * (prob_grads[index] - dots) * SCALE).astype(BF16))
             halves.append(prob.astype(BF16))
-        dv = [nt(att_grad[band, :], half).astype(BF16) for band, half in zip(bands, halves)]
-        key_t = k_t[ball]
-        dq = [nn(key_t[band, :], part).astype(BF16) for band, part in zip(bands, score_grads)]
-        query_t = q_t[ball]
-        dk = [nt(query_t[band, :], part).astype(BF16) for band, part in zip(bands, score_grads)]
-        all_grads = jnp.concatenate(dq + dk + dv, axis=0)
+        dv = [
+            nt(att_grad[band, sides[side]], half).astype(BF16) for (side, band), half in zip(pieces, halves)
+        ]
+        dq = [
+            nn(k_t[2 * step + side, band, :], part).astype(BF16)
+            for (side, band), part in zip(pieces, score_grads)
+        ]
+        dk = [
+            nt(q_t[2 * step + side, band, :], part).astype(BF16)
+            for (side, band), part in zip(pieces, score_grads)
+        ]
+        all_grads = jnp.concatenate(
+            [
+                jnp.concatenate(dq[:HEADS] + dk[:HEADS] + dv[:HEADS], axis=0),
+                jnp.concatenate(dq[HEADS:] + dk[HEADS:] + dv[HEADS:], axis=0),
+            ],
+            axis=1,
+        )
         normed_grad = nn(wcat[...], all_grads)
         acc_t[0:768, :] += nn(all_grads, nrm[rows, :])
         scaled_grad = jnp.transpose(normed_grad) * gain
@@ -361,11 +387,13 @@
         ).astype(BF16)
         gstage[0, rows, :] = ordered_grad[:, :LOCAL]
         gstage[1, rows, :] = ordered_grad[:, LOCAL:]
-        grad_copy(ball).start()
-        grads[ours(ball), :] = gstage[pl.ds(c, 1), rows, :][0]
+        for side in range(2):
+            grad_copy(2 * step + side).start()
+        own = pl.ds(pl.multiple_of(c * HALF + step * 2 * BALL, 2 * BALL), 2 * BALL)
+        grads[own, :] = gstage[pl.ds(c, 1), rows, :][0]
         return carry
 
-    lax.fori_loop(0, BALLS, backward, 0)
+    lax.fori_loop(0, BALLS // 2, backward, 0)
 
     for index in range(3):
         part = jnp.transpose(acc_t[index * 256:(index + 1) * 256, :])
@@ -381,6 +409,41 @@
     copy_a = send(acc.at[:, given], recv_a, s_a, 0, sibling)
     copy_a.start()
 
+    tiles = ROWS // LOCAL
+    lanes = lax.broadcasted_iota(jnp.int32, (1, LOCAL), 1)
+    high_ids = lax.broadcasted_iota(jnp.int32, (tiles, LOCAL), 0)
+    low_ids = lax.broadcasted_iota(jnp.int32, (LOCAL, LOCAL), 0)
+    high_hits, low_hits = [], []
+    for tile in range(tiles):
+        target = order_rows[tile:tile + 1, :]
+        high_hits.append(jnp.where(high_ids == target // LOCAL, 1.0, 0.0).astype(BF16))
+        hit = low_ids == target % LOCAL
+        source = lanes + tile * LOCAL
+        low_hits.append(
+            jnp.concatenate(
+                [
+                    jnp.where(hit, (source // 64).astype(F32), 0.0),
+                    jnp.where(hit, (source % 64).astype(F32), 0.0),
+                ],
+                axis=0,
+            ).astype(BF16)
+        )
+    found = nt(jnp.concatenate(high_hits, axis=1), jnp.concatenate(low_hits, axis=1))
+    inverse_order = (found[:, :LOCAL] * 64.0 + found[:, LOCAL:]).astype(jnp.int32)
+    places[...] = jnp.clip(inverse_order, 0, ROWS - 1)
+    fetch = pltpu.make_async_copy(places, places_smem, s_places)
+    fetch.start()
+
+    def return_rows(start, stop):
+        def step(block, carry):
+            for inner in range(16):
+                row = places_smem[block // 8, (block % 8) * 16 + inner]
+                moved[pl.ds(block * 16 + inner, 1), :] = wide[pl.ds(row, 1), :]
+            return carry
+
+        lax.fori_loop(start // 16, stop // 16, step, 0)
+        point_grad[start:stop, :] = moved[start:stop, :].astype(BF16)
+
     def their_mixed(ball, carry):
         rows = here(ball)
         proj_copy(ball).wait_recv()
@@ -392,18 +455,22 @@
 
     copy_a.wait_recv()
     sum_a[...] = acc[:, kept, :] + recv_a[...]
+    half_a[...] = sum_a[...].astype(BF16)
 
     def copy_c(distance):
         piece = pl.ds(pl.multiple_of(plane_index(distance) * 32, 32), 32)
-        return send(sum_a.at[:, piece], recv_c.at[distance], s_c, distance, plane_peer(distance))
+        return send(half_a.at[:, piece], recv_c.at[distance], s_c, distance, plane_peer(distance))
 
     for distance in range(1, 16):
         copy_c(distance).start()
     lax.fori_loop(0, BALLS, their_mixed, 0)
+    for ball in range(BALLS):
+        grad_copy(ball).wait_recv()
+    wide[...] = grads[...].astype(F32)
     part = sum_a[:, pl.ds(pl.multiple_of(plane * 32, 32), 32), :]
     for distance in range(1, 16):
         copy_c(distance).wait_recv()
-        part = part + recv_c[distance]
+        part = part + recv_c[distance].astype(F32)
     sum_c[...] = part
 
     def copy_z(distance):
@@ -412,6 +479,8 @@
     for distance in range(1, 8):
         copy_z(distance).start()
     recv_z[pl.ds(ring, 1)] = sum_c[pl.ds(c, 1)]
+    fetch.wait()
+    return_rows(0, HALF)
     for distance in range(1, 8):
         copy_z(distance).wait_recv()
     part = recv_z[0]
@@ -425,6 +494,7 @@
 
     for distance in range(1, 16):
         copy_f(distance).start()
+    return_rows(HALF, ROWS)
     for distance in range(1, 16):
         copy_f(distance).wait_recv()
 
@@ -444,15 +514,18 @@
         points_copy(ball).wait_send()
         cot_copy(ball).wait_send()
         proj_copy(ball).wait_send()
-        grad_copy(ball).wait()
+        grad_copy(ball).wait_send()
         return carry
 
     lax.fori_loop(0, BALLS, settle, 0)
-    for distance in range(1, 32):
+    tree_first().wait_send()
+    early_first().wait_send()
+    for distance in range(1, 8):
+        early_copy(distance).wait_send()
+    for distance in range(1, 16):
         tree_copy(distance).wait_send()
     copy_a.wait_send()
     for distance in range(1, 16):
-        early_copy(distance).wait_send()
         copy_c(distance).wait_send()
         copy_f(distance).wait_send()
     for distance in range(1, 8):
@@ -460,7 +533,7 @@
     copy_g.wait_send()
 
 
-def run_main(order, points, cot, gain, tree_gain, slots, w, wo):
+def run_main(order, order_rows, points, cot, gain, tree_gain, slots, w, wo):
     vmem = pl.BlockSpec(memory_space=pltpu.VMEM)
     sems = lambda count: pltpu.SemaphoreType.DMA((2, count))
     v = pltpu.VMEM
@@ -472,7 +545,7 @@
             jax.ShapeDtypeStruct((3, WIDTH, LOCAL), F32),
             jax.ShapeDtypeStruct((LOCAL, WIDTH), F32),
         ),
-        in_specs=[pl.BlockSpec(memory_space=pltpu.SMEM)] + [vmem] * 7,
+        in_specs=[pl.BlockSpec(memory_space=pltpu.SMEM)] + [vmem] * 8,
         out_specs=(vmem,) * 4,
         scratch_shapes=[
             v((ROWS, LOCAL), F32),
@@ -486,14 +559,14 @@
             v((HALF, WIDTH), BF16),
             v((BALLS, WIDTH, BALL), BF16),
             v((BALLS, WIDTH, BALL), BF16),
-            v((BALLS, WIDTH, BALL), BF16),
+            v((BALLS // 2, WIDTH, 2 * BALL), BF16),
             v((HALF, WIDTH), BF16),
             v((2, HALF, LOCAL), F32),
             v((HALF, LOCAL), F32),
             v((BALLS * HEADS, BALL, BALL), F32),
-            v((256, 2 * LOCAL), F32),
-            v((2, BALLS, LOCAL), F32),
-            v((256, LOCAL), F32),
+            v((2, LOCAL, 2 * LOCAL), F32),
+            v((2, 16, LOCAL), F32),
+            v((2, LOCAL, LOCAL), F32),
             v((LEVELS, 256, 256), BF16),
             v((LEVELS, 256, 256), BF16),
             v((256, LOCAL), F32),
@@ -506,27 +579,31 @@
             v((2, 1024, LOCAL), F32),
             v((2, 512, LOCAL), F32),
             v((2, 512, LOCAL), F32),
-            v((16, 2, 32, LOCAL), F32),
+            v((2, 512, LOCAL), BF16),
+            v((16, 2, 32, LOCAL), BF16),
             v((2, 32, LOCAL), F32),
             v((8, 32, LOCAL), F32),
             v((512, LOCAL), F32),
             v((1024, LOCAL), F32),
-            sems(1), sems(BALLS), sems(BALLS), sems(BALLS), sems(BALLS), sems(16), sems(32),
+            v((ROWS, LOCAL), BF16),
+            v((ROWS // LOCAL, LOCAL), jnp.int32),
+            pltpu.SMEM((ROWS // LOCAL, LOCAL), jnp.int32),
+            pltpu.SemaphoreType.DMA,
+            sems(1), sems(BALLS), sems(BALLS), sems(BALLS), sems(BALLS), sems(8), sems(16),
             sems(1), sems(1), sems(16), sems(8), sems(16), sems(1),
         ],
         compiler_params=pltpu.CompilerParams(
             collective_id=0, has_side_effects=True, vmem_limit_bytes=58 * 1024 * 1024
         ),
         cost_estimate=pl.CostEstimate(flops=8 * 10**9, bytes_accessed=8 * 10**6, transcendentals=4 * 10**6),
-    )(order, points, cot, gain, tree_gain, slots, w, wo)
+    )(order, order_rows, points, cot, gain, tree_gain, slots, w, wo)
 
 
 def local(points, order, norm_gain, qkv_weight, out_weight, tree_gain, partner_slot, cotangent):
-    mixed, grads, qkv_total, out_total = run_main(
-        order, points, cotangent, norm_gain[None], tree_gain, partner_slot, qkv_weight, out_weight
+    return run_main(
+        order, order.reshape(ROWS // LOCAL, LOCAL), points, cotangent, norm_gain[None], tree_gain,
+        partner_slot.T, qkv_weight, out_weight,
     )
-    point_grad = permute_rows(scatter_kernel, order, grads)
-    return (mixed, point_grad, qkv_total, out_total)
 
 
 def solution(mesh):

time: 96.9 us -> 84.5 us (0.87)
  Pallas kernels: 90.5 us -> 78.3 us
    pallas_call x1 -> x0, Pallas kernels: 6.45 us -> none  [permute_rows(): pl.pallas_call(kernel, out_shape=jax.ShapeDtypeStruct((ROWS, LOCAL), BF16...]
    pallas_call x1, Pallas kernels: 84.1 us -> 78.3 us  [run_main(): pl.pallas_call(main_kernel, out_shape=(jax.ShapeDtypeStruct((ROWS, LOCAL)...]
    unnamed x14 -> x10, local copies, waits for them, and re-layouts: 5.49 us -> 5.26 us
where the time goes in v3:
time: 84.5 us; the launch traced here: 84.2 us
  Pallas kernels  78.3 us (93%)
  local copies, waits for them, and re-layouts  5.26 us (6%)
    pallas_call x1, Pallas kernels, run_main(): pl.pallas_call(main_kernel, out_shape=(jax.ShapeDtypeStruct((ROWS, LOCAL)...  78.3 us
    unnamed x10, local copies, waits for them, and re-layouts  5.26 us

profile of v3, /device:TPU:1, one launch (start us, length us, event | category | flops | bytes accessed | tf_op | source)
XLA Modules:
  0.0 84.2 jit_solution(13748823374415880987)
XLA Ops:
  0.6 78.3 %shard_map.111 = (bf16[4096,128]{1,0:T(8,128)(2,1)}, bf16[4096,128]{1,0:T(8,128)(2,1)}, f32[3,256,128]{2,1,0:T(8,128)}, f32[128,256]{1,0:T(8,128)}) custom-call(s32[4096]{0:T(1024)} %order_ref.1, s32[32,128]{1,0:T(8,128)} %bitcast.3, bf16[4096,128]{1,0:T(8,128)(2,1)} %points.1, bf16[4096,128]{1,0:T(8,128)(2,1)} %cot.1, f32[1,128]{1,0:T(1,128)} %bitcast.5, ...), custom_call_target="tpu_custom_call" | custom-call | flops 8000000000 | bytes 8000000 | tf_op jit(solution)/shard_map/pallas_call | solution.py:540
  79.0 0.0 copy-start
  79.0 2.4 %copy.16 = bf16[4096,128]{1,0:T(8,128)(2,1)} copy(bf16[4096,128]{1,0:T(8,128)(2,1)} %get-tuple-element.8) | data formatting | bytes 2097152
  81.3 0.0 copy-done
  81.3 0.0 copy-start.1
  81.3 1.0 %copy.17 = bf16[4096,128]{1,0:T(8,128)(2,1)} copy(bf16[4096,128]{1,0:T(8,128)(2,1)S(1)} %copy-done) | data formatting | bytes 2097152
  82.3 0.3 copy-done.1
  82.6 0.0 copy-start.2
  82.6 0.7 copy.18
  83.3 0.3 copy-done.2
  83.6 0.7 copy.19
Async XLA Ops:
  79.0 2.4 %copy-start = (bf16[4096,128]{1,0:T(8,128)(2,1)S(1)}, bf16[4096,128]{1,0:T(8,128)(2,1)}, u32[]{:S(2)}) copy-start(bf16[4096,128]{1,0:T(8,128)(2,1)} %get-tuple-element.9) | copy-start | bytes 3145732
  81.3 1.2 %copy-start.1 = (f32[3,256,128]{2,1,0:T(8,128)S(1)}, f32[3,256,128]{2,1,0:T(8,128)}, u32[]{:S(2)}) copy-start(f32[3,256,128]{2,1,0:T(8,128)} %get-tuple-element.10) | copy-start | bytes 1179652
  82.6 1.0 %copy-start.2 = (f32[128,256]{1,0:T(8,128)S(1)}, f32[128,256]{1,0:T(8,128)}, u32[]{:S(2)}) copy-start(f32[128,256]{1,0:T(8,128)} %get-tuple-element.11) | copy-start | bytes 393220

commit v4 on v3

--- a/solution.py
+++ b/solution.py
@@ -19,7 +19,7 @@
 HEADS = 8
 BALLS = 8
 GROUP = 16
-EARLY_COT = 4
+EARLY_COT = 6
 
 F32 = jnp.float32
 BF16 = jnp.bfloat16
@@ -453,6 +453,22 @@
         ).astype(BF16)
         return carry
 
+    small_copy().wait_send()
+    ng_copy().wait_send()
+
+    def settle_early(ball, carry):
+        points_copy(ball).wait_send()
+        cot_copy(ball).wait_send()
+        return carry
+
+    lax.fori_loop(0, BALLS, settle_early, 0)
+    tree_first().wait_send()
+    early_first().wait_send()
+    for distance in range(1, 8):
+        early_copy(distance).wait_send()
+    for distance in range(1, 16):
+        tree_copy(distance).wait_send()
+
     copy_a.wait_recv()
     sum_a[...] = acc[:, kept, :] + recv_a[...]
     half_a[...] = sum_a[...].astype(BF16)
@@ -479,6 +495,8 @@
     for distance in range(1, 8):
         copy_z(distance).start()
     recv_z[pl.ds(ring, 1)] = sum_c[pl.ds(c, 1)]
+    for distance in range(1, 16):
+        copy_c(distance).wait_send()
     fetch.wait()
     return_rows(0, HALF)
     for distance in range(1, 8):
@@ -507,26 +525,14 @@
     out_out[:, :LOCAL] = total[768:896, :]
     out_out[:, LOCAL:] = total[896:1024, :]
 
-    small_copy().wait_send()
-    ng_copy().wait_send()
-
     def settle(ball, carry):
-        points_copy(ball).wait_send()
-        cot_copy(ball).wait_send()
         proj_copy(ball).wait_send()
         grad_copy(ball).wait_send()
         return carry
 
     lax.fori_loop(0, BALLS, settle, 0)
-    tree_first().wait_send()
-    early_first().wait_send()
-    for distance in range(1, 8):
-        early_copy(distance).wait_send()
-    for distance in range(1, 16):
-        tree_copy(distance).wait_send()
     copy_a.wait_send()
     for distance in range(1, 16):
-        copy_c(distance).wait_send()
         copy_f(distance).wait_send()
     for distance in range(1, 8):
         copy_z(distance).wait_send()

time: 84.5 us -> 87.7 us (1.038)
  Pallas kernels: 78.3 us -> 81.6 us
    pallas_call x1, Pallas kernels: 78.3 us -> 81.6 us  [run_main(): pl.pallas_call(main_kernel, out_shape=(jax.ShapeDtypeStruct((ROWS, LOCAL)...]
where the time goes in v4:
time: 87.7 us; the launch traced here: 87.5 us
  Pallas kernels  81.6 us (93%)
  local copies, waits for them, and re-layouts  5.26 us (6%)
    pallas_call x1, Pallas kernels, run_main(): pl.pallas_call(main_kernel, out_shape=(jax.ShapeDtypeStruct((ROWS, LOCAL)...  81.6 us
    unnamed x10, local copies, waits for them, and re-layouts  5.26 us

profile of v4, /device:TPU:1, one launch (start us, length us, event | category | flops | bytes accessed | tf_op | source)
XLA Modules:
  0.0 87.5 jit_solution(12243240571716716810)
XLA Ops:
  0.6 81.6 %shard_map.111 = (bf16[4096,128]{1,0:T(8,128)(2,1)}, bf16[4096,128]{1,0:T(8,128)(2,1)}, f32[3,256,128]{2,1,0:T(8,128)}, f32[128,256]{1,0:T(8,128)}) custom-call(s32[4096]{0:T(1024)} %order_ref.1, s32[32,128]{1,0:T(8,128)} %bitcast.3, bf16[4096,128]{1,0:T(8,128)(2,1)} %points.1, bf16[4096,128]{1,0:T(8,128)(2,1)} %cot.1, f32[1,128]{1,0:T(1,128)} %bitcast.5, ...), custom_call_target="tpu_custom_call" | custom-call | flops 8000000000 | bytes 8000000 | tf_op jit(solution)/shard_map/pallas_call | solution.py:546
  82.2 0.0 copy-start
  82.2 2.4 %copy.16 = bf16[4096,128]{1,0:T(8,128)(2,1)} copy(bf16[4096,128]{1,0:T(8,128)(2,1)} %get-tuple-element.8) | data formatting | bytes 2097152
  84.6 0.0 copy-done
  84.6 0.0 copy-start.1
  84.6 1.0 %copy.17 = bf16[4096,128]{1,0:T(8,128)(2,1)} copy(bf16[4096,128]{1,0:T(8,128)(2,1)S(1)} %copy-done) | data formatting | bytes 2097152
  85.5 0.3 copy-done.1
  85.8 0.0 copy-start.2
  85.8 0.7 copy.18
  86.5 0.3 copy-done.2
  86.8 0.7 copy.19
Async XLA Ops:
  82.2 2.4 %copy-start = (bf16[4096,128]{1,0:T(8,128)(2,1)S(1)}, bf16[4096,128]{1,0:T(8,128)(2,1)}, u32[]{:S(2)}) copy-start(bf16[4096,128]{1,0:T(8,128)(2,1)} %get-tuple-element.9) | copy-start | bytes 3145732
  84.6 1.2 %copy-start.1 = (f32[3,256,128]{2,1,0:T(8,128)S(1)}, f32[3,256,128]{2,1,0:T(8,128)}, u32[]{:S(2)}) copy-start(f32[3,256,128]{2,1,0:T(8,128)} %get-tuple-element.10) | copy-start | bytes 1179652
  85.8 1.0 %copy-start.2 = (f32[128,256]{1,0:T(8,128)S(1)}, f32[128,256]{1,0:T(8,128)}, u32[]{:S(2)}) copy-start(f32[128,256]{1,0:T(8,128)} %get-tuple-element.11) | copy-start | bytes 393220

commit v5 on v3

--- a/solution.py
+++ b/solution.py
@@ -464,21 +464,21 @@
     for distance in range(1, 16):
         copy_c(distance).start()
     lax.fori_loop(0, BALLS, their_mixed, 0)
+    part = sum_a[:, pl.ds(pl.multiple_of(plane * 32, 32), 32), :]
+    for distance in range(1, 16):
+        copy_c(distance).wait_recv()
+        part = part + recv_c[distance].astype(F32)
+    sum_c[...] = part
+
+    def copy_z(distance):
+        return send(sum_c.at[(ring + distance) % 2], recv_z.at[ring], s_z, distance, ring_peer(distance))
+
+    for distance in range(1, 8):
+        copy_z(distance).start()
+    recv_z[pl.ds(ring, 1)] = sum_c[pl.ds(c, 1)]
     for ball in range(BALLS):
         grad_copy(ball).wait_recv()
     wide[...] = grads[...].astype(F32)
-    part = sum_a[:, pl.ds(pl.multiple_of(plane * 32, 32), 32), :]
-    for distance in range(1, 16):
-        copy_c(distance).wait_recv()
-        part = part + recv_c[distance].astype(F32)
-    sum_c[...] = part
-
-    def copy_z(distance):
-        return send(sum_c.at[(ring + distance) % 2], recv_z.at[ring], s_z, distance, ring_peer(distance))
-
-    for distance in range(1, 8):
-        copy_z(distance).start()
-    recv_z[pl.ds(ring, 1)] = sum_c[pl.ds(c, 1)]
     fetch.wait()
     return_rows(0, HALF)
     for distance in range(1, 8):
@@ -495,6 +495,24 @@
     for distance in range(1, 16):
         copy_f(distance).start()
     return_rows(HALF, ROWS)
+
+    small_copy().wait_send()
+    ng_copy().wait_send()
+
+    def settle_early(ball, carry):
+        points_copy(ball).wait_send()
+        cot_copy(ball).wait_send()
+        return carry
+
+    lax.fori_loop(0, BALLS, settle_early, 0)
+    tree_first().wait_send()
+    early_first().wait_send()
+    for distance in range(1, 8):
+        early_copy(distance).wait_send()
+    for distance in range(1, 16):
+        tree_copy(distance).wait_send()
+        copy_c(distance).wait_send()
+
     for distance in range(1, 16):
         copy_f(distance).wait_recv()
 
@@ -507,26 +525,14 @@
     out_out[:, :LOCAL] = total[768:896, :]
     out_out[:, LOCAL:] = total[896:1024, :]
 
-    small_copy().wait_send()
-    ng_copy().wait_send()
-
     def settle(ball, carry):
-        points_copy(ball).wait_send()
-        cot_copy(ball).wait_send()
         proj_copy(ball).wait_send()
         grad_copy(ball).wait_send()
         return carry
 
     lax.fori_loop(0, BALLS, settle, 0)
-    tree_first().wait_send()
-    early_first().wait_send()
-    for distance in range(1, 8):
-        early_copy(distance).wait_send()
-    for distance in range(1, 16):
-        tree_copy(distance).wait_send()
     copy_a.wait_send()
     for distance in range(1, 16):
-        copy_c(distance).wait_send()
         copy_f(distance).wait_send()
     for distance in range(1, 8):
         copy_z(distance).wait_send()

time: 84.5 us -> 84.6 us (level)
  no operation moved by 1% of the time
where the time goes in v5:
time: 84.6 us; the launch traced here: 84.4 us
  Pallas kernels  78.5 us (93%)
  local copies, waits for them, and re-layouts  5.26 us (6%)
    pallas_call x1, Pallas kernels, run_main(): pl.pallas_call(main_kernel, out_shape=(jax.ShapeDtypeStruct((ROWS, LOCAL)...  78.5 us
    unnamed x10, local copies, waits for them, and re-layouts  5.26 us

profile of v5, /device:TPU:1, one launch (start us, length us, event | category | flops | bytes accessed | tf_op | source)
XLA Modules:
  0.0 84.4 jit_solution(711540381616222908)
XLA Ops:
  0.6 78.5 %shard_map.111 = (bf16[4096,128]{1,0:T(8,128)(2,1)}, bf16[4096,128]{1,0:T(8,128)(2,1)}, f32[3,256,128]{2,1,0:T(8,128)}, f32[128,256]{1,0:T(8,128)}) custom-call(s32[4096]{0:T(1024)} %order_ref.1, s32[32,128]{1,0:T(8,128)} %bitcast.3, bf16[4096,128]{1,0:T(8,128)(2,1)} %points.1, bf16[4096,128]{1,0:T(8,128)(2,1)} %cot.1, f32[1,128]{1,0:T(1,128)} %bitcast.5, ...), custom_call_target="tpu_custom_call" | custom-call | flops 8000000000 | bytes 8000000 | tf_op jit(solution)/shard_map/pallas_call | solution.py:546
  79.1 0.0 copy-start
  79.1 2.4 %copy.16 = bf16[4096,128]{1,0:T(8,128)(2,1)} copy(bf16[4096,128]{1,0:T(8,128)(2,1)} %get-tuple-element.8) | data formatting | bytes 2097152
  81.5 0.0 copy-done
  81.5 0.0 copy-start.1
  81.5 1.0 %copy.17 = bf16[4096,128]{1,0:T(8,128)(2,1)} copy(bf16[4096,128]{1,0:T(8,128)(2,1)S(1)} %copy-done) | data formatting | bytes 2097152
  82.4 0.3 copy-done.1
  82.7 0.0 copy-start.2
  82.7 0.7 copy.18
  83.4 0.3 copy-done.2
  83.7 0.7 copy.19
Async XLA Ops:
  79.1 2.4 %copy-start = (bf16[4096,128]{1,0:T(8,128)(2,1)S(1)}, bf16[4096,128]{1,0:T(8,128)(2,1)}, u32[]{:S(2)}) copy-start(bf16[4096,128]{1,0:T(8,128)(2,1)} %get-tuple-element.9) | copy-start | bytes 3145732
  81.5 1.2 %copy-start.1 = (f32[3,256,128]{2,1,0:T(8,128)S(1)}, f32[3,256,128]{2,1,0:T(8,128)}, u32[]{:S(2)}) copy-start(f32[3,256,128]{2,1,0:T(8,128)} %get-tuple-element.10) | copy-start | bytes 1179652
  82.7 1.0 %copy-start.2 = (f32[128,256]{1,0:T(8,128)S(1)}, f32[128,256]{1,0:T(8,128)}, u32[]{:S(2)}) copy-start(f32[128,256]{1,0:T(8,128)} %get-tuple-element.11) | copy-start | bytes 393220
